TPU v7x, 32 devices: a whole 2x2x4 slice. The times are simulated.
32 devices in a mesh: grp: 2 (over y), keys: 4 (over x, core), qry: 4 (over z).
Axes of the slice: x: 2, y: 2, z: 4, core: 2. Of those that a mesh axis runs over, the one named last changes fastest.
Arguments:
- queries: bfloat16 [4096, 8, 128], P(('grp', 'keys', 'qry')), parts along dimension 0, may hold values from -40 to 40, as said below
- cache_keys: bfloat16 [4096, 128], P(('grp', 'keys')), parts along dimension 0, may hold values from -128 to 128, as said below
- cache_values: bfloat16 [4096, 128], P(('grp', 'keys')), parts along dimension 0, may hold values from -24 to 24
- entry: int32 [8, 4], P(('grp', 'keys'), 'qry'), parts along dimension 0, may hold values from 0 to 3
- visits: int32 [8, 4], P(('grp', 'keys'), 'qry'), parts along dimension 0, may hold values from 3 to 4
- doc_length: int32 [2], P('grp'), parts along dimension 0, may hold values from 1025 to 2048
- slot_params: float32 [2048, 256], P(('grp', 'keys', 'qry')), parts along dimension 0, may hold values from -128 to 128, as said below
- first_moment: float32 [2048, 256], P(('grp', 'keys', 'qry')), parts along dimension 0, may hold values from -3 to 3
- second_moment: float32 [2048, 256], P(('grp', 'keys', 'qry')), parts along dimension 0, may hold values from 0.05 to 1
Outputs:
- teacher_out: bfloat16 [4096, 8, 128], P(('grp', 'keys', 'qry')), parts along dimension 0
- slot_grad: float32 [2048, 256], P(('grp', 'keys', 'qry')), parts along dimension 0
- new_params: float32 [2048, 256], P(('grp', 'keys', 'qry')), parts along dimension 0
- new_first: float32 [2048, 256], P(('grp', 'keys', 'qry')), parts along dimension 0
- new_second: float32 [2048, 256], P(('grp', 'keys', 'qry')), parts along dimension 0
- loss: float32 [2], P('grp'), parts along dimension 0
There are 2 independent parts, one for each index of `grp`. A program takes and returns all parts, laid end to end along the dimension named above; each array names one. Nothing has to cross between parts.
Inputs may be any that keep to these rules, and one draw needn't show every extreme that they name: `queries`: query entries stay within the stated range. `cache_keys`: cache key entries stay within the stated range. `slot_params`: slot entries stay within the stated range.
All inputs are finite; a program needn't handle non-finite values.
Results may differ from a plain program's by a relative error of at most 0.0045.
Values may be sent and summed in bfloat16 or wider, within the bound.
A program may use at most 64 MiB of HBM per device.

v0:
```python
import math

import jax
import jax.numpy as jnp
from jax import lax
from jax.sharding import PartitionSpec as P

NEG = -1e30


def shifted(block, axis, distance):
    devices = range(lax.axis_size(axis))
    route = [((i - distance) % len(devices), i) for i in devices]
    return lax.ppermute(block, axis, route)


def row_scores(left, right):
    return lax.dot_general(
        left, right, (((1,), (1,)), ((), ())), preferred_element_type=jnp.float32
    )


def attend(state, query_blocks, keys, values, shard, length, score_scale):
    block_width = keys.shape[0]
    place = shard * block_width + lax.iota(jnp.int32, block_width)
    live = (place < length)[None, :]

    def one(block_entry):
        query_portion, big, total, acc = block_entry
        logit_score = jnp.where(live, row_scores(query_portion, keys) * score_scale, NEG)
        new_big = jnp.maximum(big, jnp.max(logit_score, axis=1))
        weight = jnp.where(live, jnp.exp(logit_score - new_big[:, None]), 0.0)
        fade = jnp.exp(big - new_big)
        total = total * fade + jnp.sum(weight, axis=1)
        acc = acc * fade[:, None] + jnp.dot(
            weight.astype(jnp.bfloat16), values, preferred_element_type=jnp.float32
        )
        return (new_big, total, acc)

    big, total, acc = state
    return lax.map(one, (query_blocks, big, total, acc))


def student_tile(loop_state, block_entry, student_keys, student_values, score_scale):
    key_gradient, squared_terms = loop_state
    query_portion, target = block_entry
    logit_score = row_scores(query_portion, student_keys) * score_scale
    peak = jnp.max(logit_score, axis=1, keepdims=True)
    weight = jnp.exp(logit_score - peak)
    prob = weight / jnp.sum(weight, axis=1, keepdims=True)
    block_prob = prob.astype(jnp.bfloat16)
    student_output = jnp.dot(block_prob, student_values, preferred_element_type=jnp.float32)
    diff = student_output - target.astype(jnp.float32)
    squared_terms = squared_terms + jnp.sum(diff * diff)
    block_difference = diff.astype(jnp.bfloat16)
    prob_gradient = row_scores(block_difference, student_values)
    inner = jnp.sum(prob * prob_gradient, axis=1, keepdims=True)
    dscore = (prob * (prob_gradient - inner) * score_scale).astype(jnp.bfloat16)
    dkeys = lax.dot_general(
        dscore, query_portion, (((0,), (0,)), ((), ())), preferred_element_type=jnp.float32
    )
    dvals = lax.dot_general(
        block_prob, block_difference, (((0,), (0,)), ((), ())), preferred_element_type=jnp.float32
    )
    key_gradient = key_gradient + jnp.concatenate([dkeys, dvals], axis=1)
    return ((key_gradient, squared_terms), None)


def body(
    queries,
    cache_keys,
    cache_values,
    entry,
    visits,
    doc_length,
    slot_params,
    first_moment,
    second_moment,
):
    shards = lax.axis_size("keys")
    me = lax.axis_index("keys")
    tok, heads, block_width = queries.shape
    rows = tok * heads
    block = math.gcd(rows, 512)
    nblocks = rows // block
    score_scale = 1.0 / math.sqrt(block_width)
    length = doc_length[0]
    query_blocks = queries.reshape(nblocks, block, block_width)
    start = entry[0, 0]
    count = visits[0, 0]
    state = (
        jnp.full((nblocks, block), NEG, jnp.float32),
        jnp.zeros((nblocks, block), jnp.float32),
        jnp.zeros((nblocks, block, block_width), jnp.float32),
    )

    def visit(step, keys, values, loop_state):
        held = jnp.remainder(me - step, shards)
        go = jnp.remainder(-step - start, shards) < count
        return lax.cond(
            go,
            lambda column_index: attend(
                column_index, query_blocks, keys, values, held, length, score_scale
            ),
            lambda column_index: column_index,
            loop_state,
        )

    def turn(step, loop_state):
        keys, values, big, total, acc = loop_state
        big, total, acc = visit(step, keys, values, (big, total, acc))
        keys, values = shifted((keys, values), "keys", 1)
        return (keys, values, big, total, acc)

    keys, values, big, total, acc = lax.fori_loop(
        0, shards - 1, turn, (cache_keys, cache_values) + state
    )
    big, total, acc = visit(shards - 1, keys, values, (big, total, acc))
    teacher_block_list = (acc / total[:, :, None]).astype(jnp.bfloat16)
    teacher_out = teacher_block_list.reshape(tok, heads, block_width)
    copies = slot_params.astype(jnp.bfloat16)
    complete_sum = lax.all_gather(copies, ("keys", "qry"), axis=0, tiled=True)
    student_keys = complete_sum[:, :block_width]
    student_values = complete_sum[:, block_width:]
    initial_state = (jnp.zeros(complete_sum.shape, jnp.float32), jnp.zeros((), jnp.float32))
    (grad_terms, squared_terms), ignored_value = lax.scan(
        lambda column_index, loop_index: student_tile(
            column_index, loop_index, student_keys, student_values, score_scale
        ),
        initial_state,
        (query_blocks, teacher_block_list),
    )
    slot_grad = lax.psum_scatter(grad_terms, ("keys", "qry"), scatter_dimension=0, tiled=True)
    squares_all = lax.psum(squared_terms, ("keys", "qry"))
    loss = (squares_all / (rows * shards * lax.axis_size("qry"))).reshape(1)
    new_first = 0.9 * first_moment + 0.1 * slot_grad
    new_second = 0.95 * second_moment + 0.05 * slot_grad * slot_grad
    new_params = slot_params - 0.02 * new_first / (jnp.sqrt(new_second) + 1e-08)
    return (teacher_out, slot_grad, new_params, new_first, new_second, loss)


def solution(mesh):
    return jax.shard_map(
        body,
        mesh=mesh,
        in_specs=(
            P(("grp", "keys", "qry"), None, None),
            P(("grp", "keys"), None),
            P(("grp", "keys"), None),
            P(("grp", "keys"), "qry"),
            P(("grp", "keys"), "qry"),
            P("grp"),
            P(("grp", "keys", "qry"), None),
            P(("grp", "keys", "qry"), None),
            P(("grp", "keys", "qry"), None),
        ),
        out_specs=(
            P(("grp", "keys", "qry"), None, None),
            P(("grp", "keys", "qry"), None),
            P(("grp", "keys", "qry"), None),
            P(("grp", "keys", "qry"), None),
            P(("grp", "keys", "qry"), None),
            P("grp"),
        ),
        check_vma=False,
    )
```

profile of v0, /device:TPU:0, one launch (start us, length us, event | category | flops | bytes accessed | tf_op | source)
XLA Modules:
  0.0 162.4 jit_solution(8857728833277977669)
XLA Ops:
  8.6 0.8 convert_element_type.42
  9.5 38.8 %all_gather.3 = bf16[1024,256]{1,0:T(8,128)(2,1)S(1)} all-gather(bf16[64,256]{1,0:T(8,128)(2,1)S(1)} %convert_element_type.42), channel_id=1, replica_groups=mesh['grp'=2,'keys'=4,'qry'=4] {'keys','qry'}, dimensions={0}, use_global_device_ids=true | all-gather | bytes 557056 | tf_op jit(solution)/shard_map/all_gather | solution.py:122
  48.4 34.0 %while.82 = (s32[]{:T(128)}, bf16[512,128]{1,0:T(8,128)(2,1)S(1)}, bf16[512,128]{1,0:T(8,128)(2,1)S(1)}, f32[2,512]{1,0:T(2,128)S(1)}, f32[2,512]{1,0:T(2,128)S(...) while((s32[]{:T(128)}, bf16[512,128]{1,0:T(8,128)(2,1)S(1)}, ...), condition=%wide.region_7.8_spmd, body=%wide.region_0.7_spmd.sunk | while | flops 136711200 | bytes 6747030 | solution.py:115
  48.5 0.7 copy.55
  49.1 0.6 copy.56
  49.8 1.3 collective-permute-start.1
  52.4 7.5 %conditional.4 = ((f32[2,512]{1,0:T(2,128)S(1)}, f32[2,512]{1,0:T(2,128)S(1)}, f32[2,512,128]{2,1,0:T(8,128)S(1)})) conditional(s32[]{:T(128)} %convert_element_type.75, (f32[2,512]{1,0:T(2,128)S(1)}, f32[2,512]{1,0:T(2,128)S(1)}, f32[2,512,128]{2,1,0:T(8,128)S(1)}) %tuple.135, (s32[]{:T(128)}, s32[]{:T(128)}, s32[]{:T(128)}, f32[2,512]{1,0:T(2,128)S(1)}, ...), branch_computations={%region_1.1_spmd, %region_2.6_spmd} | conditional | flops 136711184 | bytes 5173698 | solution.py:100
  52.5 7.4 %while.80 = (s32[]{:T(128)}, f32[2,512]{1,0:T(2,128)S(1)}, f32[2,512]{1,0:T(2,128)S(1)}, f32[2,512,128]{2,1,0:T(8,128)S(1)}, f32[2,512]{1,0:T(2,128)S(1)}, /*ind...) while((s32[]{:T(128)}, f32[2,512]{1,0:T(2,128)S(1)}, ...), condition=%wide.region_6.5_spmd.clone, body=%wide.region_3.4_spmd.clone.sunk | while | flops 136711168 | bytes 4108453 | solution.py:41
  52.5 0.7 compare_reduce_fusion.4
  53.2 1.2 fusion.104
  54.4 1.4 fusion.106
  56.2 0.7 compare_reduce_fusion.4
  56.9 1.2 fusion.104
  58.1 1.4 fusion.106
  60.0 0.7 copy.55
  60.6 0.6 copy.56
  61.3 0.9 collective-permute-start.1
  63.5 7.5 %conditional.4 = ((f32[2,512]{1,0:T(2,128)S(1)}, f32[2,512]{1,0:T(2,128)S(1)}, f32[2,512,128]{2,1,0:T(8,128)S(1)})) conditional(s32[]{:T(128)} %convert_element_type.75, (f32[2,512]{1,0:T(2,128)S(1)}, f32[2,512]{1,0:T(2,128)S(1)}, f32[2,512,128]{2,1,0:T(8,128)S(1)}) %tuple.135, (s32[]{:T(128)}, s32[]{:T(128)}, s32[]{:T(128)}, f32[2,512]{1,0:T(2,128)S(1)}, ...), branch_computations={%region_1.1_spmd, %region_2.6_spmd} | conditional | flops 136711184 | bytes 5173698 | solution.py:100
  63.5 7.4 %while.80 = (s32[]{:T(128)}, f32[2,512]{1,0:T(2,128)S(1)}, f32[2,512]{1,0:T(2,128)S(1)}, f32[2,512,128]{2,1,0:T(8,128)S(1)}, f32[2,512]{1,0:T(2,128)S(1)}, /*ind...) while((s32[]{:T(128)}, f32[2,512]{1,0:T(2,128)S(1)}, ...), condition=%wide.region_6.5_spmd.clone, body=%wide.region_3.4_spmd.clone.sunk | while | flops 136711168 | bytes 4108453 | solution.py:41
  63.5 0.7 compare_reduce_fusion.4
  64.2 1.2 fusion.104
  65.5 1.4 fusion.106
  67.2 0.7 compare_reduce_fusion.4
  67.9 1.2 fusion.104
  69.2 1.4 fusion.106
  71.0 0.7 copy.55
  71.7 0.6 copy.56
  72.3 1.3 collective-permute-start.1
  75.0 7.5 %conditional.4 = ((f32[2,512]{1,0:T(2,128)S(1)}, f32[2,512]{1,0:T(2,128)S(1)}, f32[2,512,128]{2,1,0:T(8,128)S(1)})) conditional(s32[]{:T(128)} %convert_element_type.75, (f32[2,512]{1,0:T(2,128)S(1)}, f32[2,512]{1,0:T(2,128)S(1)}, f32[2,512,128]{2,1,0:T(8,128)S(1)}) %tuple.135, (s32[]{:T(128)}, s32[]{:T(128)}, s32[]{:T(128)}, f32[2,512]{1,0:T(2,128)S(1)}, ...), branch_computations={%region_1.1_spmd, %region_2.6_spmd} | conditional | flops 136711184 | bytes 5173698 | solution.py:100
  75.0 7.4 %while.80 = (s32[]{:T(128)}, f32[2,512]{1,0:T(2,128)S(1)}, f32[2,512]{1,0:T(2,128)S(1)}, f32[2,512,128]{2,1,0:T(8,128)S(1)}, f32[2,512]{1,0:T(2,128)S(1)}, /*ind...) while((s32[]{:T(128)}, f32[2,512]{1,0:T(2,128)S(1)}, ...), condition=%wide.region_6.5_spmd.clone, body=%wide.region_3.4_spmd.clone.sunk | while | flops 136711168 | bytes 4108453 | solution.py:41
  75.0 0.7 compare_reduce_fusion.4
  75.7 1.2 fusion.104
  77.0 1.4 fusion.106
  78.7 0.7 compare_reduce_fusion.4
  79.4 1.2 fusion.104
  80.7 1.4 fusion.106
  82.5 3.8 %conditional.2 = ((f32[2,512]{1,0:T(2,128)S(1)}, f32[2,512,128]{2,1,0:T(8,128)S(1)})) conditional(s32[]{:T(128)} %convert_element_type.40, (f32[2,512]{1,0:T(2,128)S(1)}, f32[2,512,128]{2,1,0:T(8,128)S(1)}) %tuple.70, (s32[]{:T(128)}, s32[]{:T(128)}, f32[2,512]{1,0:T(2,128)S(1)}, f32[2,512]{1,0:T(2,128)S(1)}, bf16[2,512,128]{2,1,0:T(8,128)(2,1)S(1)}, ...), branch_computations={%region_8.9_spmd, %region_9.14_spmd} | conditional | flops 136711184 | bytes 5159334 | solution.py:100
  82.5 3.7 %while.81 = (s32[]{:T(128)}, f32[2,512]{1,0:T(2,128)S(1)}, f32[2,512,128]{2,1,0:T(8,128)S(1)}, f32[2,512]{1,0:T(2,128)S(1)}, f32[2,512]{1,0:T(2,128)S(1)}, /*ind...) while((s32[]{:T(128)}, f32[2,512]{1,0:T(2,128)S(1)}, ...), condition=%wide.region_13.13_spmd.clone, body=%wide.region_10.12_spmd.clone.sunk | while | flops 136711168 | bytes 4102297 | solution.py:41
  82.6 0.7 compare_reduce_fusion.5
  84.4 0.7 compare_reduce_fusion.5
  86.5 10.0 %while.83 = (s32[]{:T(128)}, f32[1024,256]{0,1:T(8,128)S(1)}, f32[]{:T(128)}, bf16[2,512,128]{2,1,0:T(8,128)(2,1)S(1)}, bf16[1024,128]{1,0:T(8,128)(2,1)S(1)}, /...) while((s32[]{:T(128)}, f32[1024,256]{0,1:T(8,128)S(1)}, ...), condition=%wide.region_19.20_spmd.clone, body=%wide.region_14.19_spmd.clone.sunk | while | flops 680589824 | bytes 26753152 | solution.py:126
  87.0 0.5 fusion.97
  88.0 1.1 multiply_reduce_fusion.7
  93.0 1.1 multiply_reduce_fusion.7
  96.5 1.3 copy.15
  97.9 30.9 %psum.7 = f32[]{:T(128)} all-reduce(f32[]{:T(128)} %get-tuple-element.654), channel_id=1, replica_groups=mesh['grp'=2,'keys'=4,'qry'=4] {'keys','qry'}, use_global_device_ids=true, to_apply=%region_21.22 | all-reduce | flops 1 | bytes 8 | tf_op jit(solution)/shard_map/psum | solution.py:134
  129.5 23.4 %reduce-scatter.2.cloned.1.call-done = f32[64,256]{1,0:T(8,128)} async-done(((f32[1024,256]{1,0:T(8,128)}), f32[64,256]{1,0:T(8,128)}) %reduce-scatter.2.cloned.1.call-update) | async-done | bytes 65552 | tf_op jit(solution)/shard_map/reduce_scatter | solution.py:133
  152.9 1.5 divide_subtract_fusion
  (116 shorter events, 10.8 us)
Async XLA Ops:
  7.2 41.3 %copy-start = (bf16[128,8,128]{2,1,0:T(8,128)(2,1)S(1)}, bf16[128,8,128]{2,1,0:T(8,128)(2,1)}, u32[]{:S(2)}) copy-start(bf16[128,8,128]{2,1,0:T(8,128)(2,1)} %param.21) | copy-start | bytes 786436
  7.2 41.3 %copy-start.1 = (bf16[512,128]{1,0:T(8,128)(2,1)S(1)}, bf16[512,128]{1,0:T(8,128)(2,1)}, u32[]{:S(2)}) copy-start(bf16[512,128]{1,0:T(8,128)(2,1)} %param.22) | copy-start | bytes 393220
  7.2 41.3 %copy-start.2 = (bf16[512,128]{1,0:T(8,128)(2,1)S(1)}, bf16[512,128]{1,0:T(8,128)(2,1)}, u32[]{:S(2)}) copy-start(bf16[512,128]{1,0:T(8,128)(2,1)} %param.23) | copy-start | bytes 393220
  7.2 145.7 %reduce-scatter.2.cloned.1.call-start = ((), (), s32[]{:S(2)}) async-start(), calls=%async_computation.1 | async-start | bytes 1114112 | tf_op jit(solution)/shard_map/reduce_scatter | solution.py:133
  49.1 10.8 %collective-permute-start = (bf16[512,128]{1,0:T(8,128)(2,1)}, bf16[512,128]{1,0:T(8,128)(2,1)S(1)}, u32[]{:S(2)}, u32[]{:S(2)}) collective-permute-start(bf16[512,128]{1,0:T(8,128)(2,1)} %copy.55), channel_id=1, source_target_pairs={{12,0},{0,4},{4,8},{8,12},{13,1},{1,5},{5,9},{9,13},{14,2},{2,6},{... | collective-permute-start | bytes 393224 | tf_op jit(solution)/shard_map/while/body/eval_jaxpr/ppermute | solution.py:14
  49.8 10.2 %collective-permute-start.1 = (bf16[512,128]{1,0:T(8,128)(2,1)}, bf16[512,128]{1,0:T(8,128)(2,1)S(1)}, u32[]{:S(2)}, u32[]{:S(2)}) collective-permute-start(bf16[512,128]{1,0:T(8,128)(2,1)} %copy.56), channel_id=1, source_target_pairs={{12,0},{0,4},{4,8},{8,12},{13,1},{1,5},{5,9},{9,13},{14,2},{2,6},{... | collective-permute-start | bytes 393224 | tf_op jit(solution)/shard_map/while/body/eval_jaxpr/ppermute | solution.py:14
  60.6 10.4 %collective-permute-start = (bf16[512,128]{1,0:T(8,128)(2,1)}, bf16[512,128]{1,0:T(8,128)(2,1)S(1)}, u32[]{:S(2)}, u32[]{:S(2)}) collective-permute-start(bf16[512,128]{1,0:T(8,128)(2,1)} %copy.55), channel_id=1, source_target_pairs={{12,0},{0,4},{4,8},{8,12},{13,1},{1,5},{5,9},{9,13},{14,2},{2,6},{... | collective-permute-start | bytes 393224 | tf_op jit(solution)/shard_map/while/body/eval_jaxpr/ppermute | solution.py:14
  61.3 9.7 %collective-permute-start.1 = (bf16[512,128]{1,0:T(8,128)(2,1)}, bf16[512,128]{1,0:T(8,128)(2,1)S(1)}, u32[]{:S(2)}, u32[]{:S(2)}) collective-permute-start(bf16[512,128]{1,0:T(8,128)(2,1)} %copy.56), channel_id=1, source_target_pairs={{12,0},{0,4},{4,8},{8,12},{13,1},{1,5},{5,9},{9,13},{14,2},{2,6},{... | collective-permute-start | bytes 393224 | tf_op jit(solution)/shard_map/while/body/eval_jaxpr/ppermute | solution.py:14
  71.7 10.8 %collective-permute-start = (bf16[512,128]{1,0:T(8,128)(2,1)}, bf16[512,128]{1,0:T(8,128)(2,1)S(1)}, u32[]{:S(2)}, u32[]{:S(2)}) collective-permute-start(bf16[512,128]{1,0:T(8,128)(2,1)} %copy.55), channel_id=1, source_target_pairs={{12,0},{0,4},{4,8},{8,12},{13,1},{1,5},{5,9},{9,13},{14,2},{2,6},{... | collective-permute-start | bytes 393224 | tf_op jit(solution)/shard_map/while/body/eval_jaxpr/ppermute | solution.py:14
  72.3 10.2 %collective-permute-start.1 = (bf16[512,128]{1,0:T(8,128)(2,1)}, bf16[512,128]{1,0:T(8,128)(2,1)S(1)}, u32[]{:S(2)}, u32[]{:S(2)}) collective-permute-start(bf16[512,128]{1,0:T(8,128)(2,1)} %copy.56), channel_id=1, source_target_pairs={{12,0},{0,4},{4,8},{8,12},{13,1},{1,5},{5,9},{9,13},{14,2},{2,6},{... | collective-permute-start | bytes 393224 | tf_op jit(solution)/shard_map/while/body/eval_jaxpr/ppermute | solution.py:14
  96.5 58.0 %copy-start.3 = (bf16[2,512,128]{2,1,0:T(8,128)(2,1)}, bf16[2,512,128]{2,1,0:T(8,128)(2,1)S(1)}, u32[]{:S(2)}) copy-start(bf16[2,512,128]{2,1,0:T(8,128)(2,1)S(1)} %get-tuple-element.1306) | copy-start | bytes 786436
  96.5 56.4 %copy-start.4 = (f32[64,256]{1,0:T(8,128)S(1)}, f32[64,256]{1,0:T(8,128)}, u32[]{:S(2)}) copy-start(f32[64,256]{1,0:T(8,128)} %param.27) | copy-start | bytes 196612
  96.5 56.4 %copy-start.5 = (f32[64,256]{1,0:T(8,128)S(1)}, f32[64,256]{1,0:T(8,128)}, u32[]{:S(2)}) copy-start(f32[64,256]{1,0:T(8,128)} %param.28) | copy-start | bytes 196612
  96.5 56.4 %copy-start.6 = (f32[64,256]{1,0:T(8,128)S(1)}, f32[64,256]{1,0:T(8,128)}, u32[]{:S(2)}) copy-start(f32[64,256]{1,0:T(8,128)} %param.29) | copy-start | bytes 196612
Sparse Core Ops, SparseCore 0:
  98.0 54.8 reduce-scatter.1
where the time goes:
time: 163 us; the launch traced here: 162 us
  blocking collectives  69.8 us (43%)
  waiting for transfers between devices  23.5 us (14%)
  matrix products  23.3 us (14%)
  between operations  17.3 us (11%)
  other arithmetic  12.6 us (8%)
  loops' own time  6.18 us (4%)
  local copies, waits for them, and re-layouts  6.17 us (4%)
  starting transfers between devices  3.64 us (2%)
    all_gather x1, blocking collectives, body(): complete_sum = lax.all_gather(copies, ('keys', 'qry'), axis=0, tiled=True)  38.8 us
    psum x1, blocking collectives, body(): squares_all = lax.psum(squared_terms, ('keys', 'qry'))  30.9 us
    reduce_scatter x1, waiting for transfers between devices, body(): lax.psum_scatter(grad_terms, ('keys', 'qry'), scatter_dimension=0, tiled=...  23.4 us
    dot_general x12, matrix products, row_scores(): lax.dot_general(left, right, (((1,), (1,)), ((), ())), preferred_element_...  10.1 us
    dot_general x8, matrix products, one(): jnp.dot(weight.astype(jnp.bfloat16), values, preferred_element_type=jnp.f...  9.4 us
    lt x8, other arithmetic, attend(): live = (place < length)[None, :]  5.37 us
    another operation x1, loops' own time, body(): lax.fori_loop(0, shards - 1, turn, (cache_keys, cache_values) + state)  4.07 us
    another operation x8, local copies, waits for them, and re-layouts  3.92 us
  transfers between devices with their start and end apart: 7, of which 1 were waited for; matrix products, arithmetic and copies ran while one was open for 15% of the time, Pallas kernels for 0%

commit v1 on v0

--- a/solution.py
+++ b/solution.py
@@ -1,8 +1,11 @@
+import functools
 import math
 
 import jax
 import jax.numpy as jnp
 from jax import lax
+from jax.experimental import pallas as pl
+from jax.experimental.pallas import tpu as pltpu
 from jax.sharding import PartitionSpec as P
 
 NEG = -1e30
@@ -66,7 +69,7 @@
     return ((key_gradient, squared_terms), None)
 
 
-def body(
+def ringed(
     queries,
     cache_keys,
     cache_values,
@@ -139,6 +142,370 @@
     return (teacher_out, slot_grad, new_params, new_first, new_second, loss)
 
 
+MESH = pl.DeviceIdType.MESH
+LOW = -1e20
+LOG2E = 1.4426950408889634
+
+
+def pair_dot(left, right):
+    return lax.dot_general(
+        left, right, (((1,), (0,)), ((), ())), preferred_element_type=jnp.float32
+    )
+
+
+def step_kernel(
+    n_keys,
+    n_qry,
+    entry_ref,
+    visits_ref,
+    length_ref,
+    q_ref,
+    k_ref,
+    v_ref,
+    slot_ref,
+    first_ref,
+    second_ref,
+    teach_ref,
+    grad_ref,
+    params_ref,
+    nfirst_ref,
+    nsecond_ref,
+    loss_ref,
+    kbuf,
+    vbuf,
+    slots,
+    top,
+    acc,
+    e_ref,
+    pb_ref,
+    ds_ref,
+    student,
+    diffb,
+    gmine,
+    gsib_out,
+    gsib_in,
+    gout,
+    gin,
+    sq_own,
+    sq_sib,
+    sq_chip,
+    sq_in,
+    kv_send,
+    kv_recv,
+    sl_send,
+    sl_recv,
+    gs_send,
+    gs_recv,
+    g_send,
+    g_recv,
+    sq_send,
+    sq_recv,
+):
+    n_x = n_keys // 2
+    n_flat = n_x * n_qry
+    grp = lax.axis_index("grp")
+    me_k = lax.axis_index("keys")
+    me_q = lax.axis_index("qry")
+    x = lax.div(me_k, 2)
+    core = lax.rem(me_k, 2)
+    flat = x * n_qry + me_q
+    sibling = (grp, x * 2 + 1 - core, me_q)
+    rows, width = q_ref.shape
+    shard_len = k_ref.shape[0]
+    per = slot_ref.shape[0]
+    n_slots = slots.shape[0] * per
+    scale = 1.0 / math.sqrt(width)
+    rate = scale * LOG2E
+    tile = math.gcd(rows, 256)
+    tiles = rows // tile
+
+    def place(f, c):
+        return (lax.div(f, n_qry) * 2 + c) * n_qry + lax.rem(f, n_qry)
+
+    def peer(f):
+        return (grp, lax.div(f, n_qry) * 2 + core, lax.rem(f, n_qry))
+
+    def ahead(o):
+        return lax.rem(flat + o, n_flat)
+
+    def behind(o):
+        return lax.rem(flat + n_flat - o, n_flat)
+
+    pending = []
+
+    def send(src, dst, ssem, rsem, dev):
+        copy = pltpu.make_async_remote_copy(
+            src_ref=src, dst_ref=dst, send_sem=ssem, recv_sem=rsem,
+            device_id=dev, device_id_type=MESH,
+        )
+        copy.start()
+        pending.append(copy)
+
+    def arrived(ref, ssem, rsem):
+        pltpu.make_async_remote_copy(
+            src_ref=ref, dst_ref=ref, send_sem=ssem, recv_sem=rsem,
+            device_id=sibling, device_id_type=MESH,
+        ).wait_recv()
+
+    barrier = pltpu.get_barrier_semaphore()
+    pl.semaphore_signal(barrier, inc=1, device_id=sibling, device_id_type=MESH)
+    for o in range(1, n_flat):
+        pl.semaphore_signal(barrier, inc=1, device_id=peer(ahead(o)), device_id_type=MESH)
+    mine = place(flat, core)
+    slots[mine] = slot_ref[...].astype(jnp.bfloat16)
+    pl.semaphore_wait(barrier, n_flat)
+
+    send(slots.at[mine], slots.at[mine], sl_send.at[0], sl_recv.at[0], sibling)
+    send(k_ref, kbuf.at[0], kv_send.at[0], kv_recv.at[0], sibling)
+    send(v_ref, vbuf.at[0], kv_send.at[1], kv_recv.at[1], sibling)
+    for o in range(1, n_flat):
+        send(slots.at[mine], slots.at[mine], sl_send.at[o], sl_recv.at[o], peer(ahead(o)))
+    for j in range(1, n_x):
+        there = (grp, lax.rem(x + j, n_x) * 2 + core, me_q)
+        s = 2 * j - 1
+        send(k_ref, kbuf.at[s], kv_send.at[2 * s], kv_recv.at[2 * s], there)
+        send(v_ref, vbuf.at[s], kv_send.at[2 * s + 1], kv_recv.at[2 * s + 1], there)
+
+    start = entry_ref[0, 0]
+    count = visits_ref[0, 0]
+    length = length_ref[0]
+    ones = jnp.ones((shard_len, width), jnp.bfloat16)
+
+    def attend(keys_ref, values_ref, shard, is_first):
+        col = lax.broadcasted_iota(jnp.int32, (1, shard_len), 1) + shard * shard_len
+        turn = lax.rem(shard - me_k - start + 2 * n_keys, n_keys)
+        limit = jnp.where(turn < count, length, 0)
+        bias = jnp.where(col < limit, 0.0, NEG)
+
+        def one(t, carry):
+            at = pl.ds(pl.multiple_of(t * tile, tile), tile)
+            score = row_scores(q_ref[at, :], keys_ref[...]) + bias
+            peak = jnp.max(score, axis=1, keepdims=True)
+            values = jnp.concatenate([values_ref[...], ones], axis=1)
+            if is_first:
+                new = jnp.maximum(peak, LOW)
+                weight = jnp.exp2((score - new) * rate)
+                acc[at, :] = pair_dot(weight.astype(jnp.bfloat16), values)
+            else:
+                old = top[at, 0:1]
+                new = jnp.maximum(peak, old)
+                weight = jnp.exp2((score - new) * rate)
+                fade = jnp.exp2((old - new) * rate)
+                acc[at, :] = acc[at, :] * fade + pair_dot(weight.astype(jnp.bfloat16), values)
+            top[at, :] = jnp.broadcast_to(new, (tile, width))
+            return carry
+
+        lax.fori_loop(0, tiles, one, 0, unroll=2)
+
+    attend(k_ref, v_ref, me_k, True)
+    arrived(kbuf.at[0], kv_send.at[0], kv_recv.at[0])
+    arrived(vbuf.at[0], kv_send.at[1], kv_recv.at[1])
+    attend(kbuf.at[0], vbuf.at[0], x * 2 + 1 - core, False)
+
+    for o in range(1, n_flat):
+        block = place(behind(o), core)
+        arrived(slots.at[block], sl_send.at[o], sl_recv.at[o])
+        i = n_flat - 1 + o
+        send(slots.at[block], slots.at[block], sl_send.at[i], sl_recv.at[i], sibling)
+    arrived(slots.at[place(flat, 1 - core)], sl_send.at[0], sl_recv.at[0])
+    for o in range(1, n_flat):
+        i = n_flat - 1 + o
+        arrived(slots.at[place(behind(o), 1 - core)], sl_send.at[i], sl_recv.at[i])
+
+    def slot_keys():
+        return slots[:, :, 0:width].reshape(n_slots, width)
+
+    def slot_values():
+        return slots[:, :, width:].reshape(n_slots, width)
+
+    def grouped(value):
+        return value.reshape(slots.shape[0], per, tile)
+
+    values_t = slot_values().astype(jnp.float32).T.astype(jnp.bfloat16)
+
+    def softmax(t, carry):
+        at = pl.ds(pl.multiple_of(t * tile, tile), tile)
+        score = row_scores(slot_keys(), q_ref[at, :])
+        peak = jnp.max(score, axis=0, keepdims=True)
+        weight = jnp.exp2((score - peak) * rate)
+        prob = weight * (1.0 / jnp.sum(weight, axis=0, keepdims=True))
+        e_ref[:, :, at] = grouped(prob)
+        prob_b = prob.astype(jnp.bfloat16)
+        pb_ref[:, :, at] = grouped(prob_b)
+        student[at, :] = pair_dot(values_t, prob_b).T
+        return carry
+
+    lax.fori_loop(0, tiles, softmax, 0)
+
+    for j in range(1, n_x):
+        s = 2 * j - 1
+        arrived(kbuf.at[s], kv_send.at[2 * s], kv_recv.at[2 * s])
+        arrived(vbuf.at[s], kv_send.at[2 * s + 1], kv_recv.at[2 * s + 1])
+        g = s + 1
+        send(kbuf.at[s], kbuf.at[g], kv_send.at[2 * g], kv_recv.at[2 * g], sibling)
+        send(vbuf.at[s], vbuf.at[g], kv_send.at[2 * g + 1], kv_recv.at[2 * g + 1], sibling)
+    for j in range(1, n_x):
+        far = lax.rem(x + n_x - j, n_x) * 2
+        s = 2 * j - 1
+        attend(kbuf.at[s], vbuf.at[s], far + core, False)
+        g = s + 1
+        arrived(kbuf.at[g], kv_send.at[2 * g], kv_recv.at[2 * g])
+        arrived(vbuf.at[g], kv_send.at[2 * g + 1], kv_recv.at[2 * g + 1])
+        attend(kbuf.at[g], vbuf.at[g], far + 1 - core, False)
+
+    sq_own[...] = jnp.zeros_like(sq_own)
+
+    def differ(t, carry):
+        at = pl.ds(pl.multiple_of(t * tile, tile), tile)
+        teacher = (acc[at, 0:width] / acc[at, width:]).astype(jnp.bfloat16)
+        teach_ref[at, :] = teacher
+        diff = student[at, :] - teacher.astype(jnp.float32)
+        sq_own[...] += jnp.sum((diff * diff).reshape(tile // 8, 8, width), axis=0)
+        diff_b = diff.astype(jnp.bfloat16)
+        diffb[at, :] = diff_b
+        dprob = row_scores(slot_values(), diff_b)
+        prob = e_ref[:, :, at].reshape(n_slots, tile)
+        inner = jnp.sum(prob * dprob, axis=0, keepdims=True)
+        ds_ref[:, :, at] = grouped((prob * (dprob - inner) * scale).astype(jnp.bfloat16))
+        return carry
+
+    lax.fori_loop(0, tiles, differ, 0)
+    send(sq_own, sq_sib, sq_send.at[0], sq_recv.at[0], sibling)
+
+    order = list(range(1, n_flat)) + [0]
+    group = 2 if n_flat % 2 == 0 else 1
+    batches = [order[i:i + group] for i in range(0, n_flat, group)]
+
+    def produce(batch):
+        blocks = []
+        for o in batch:
+            blocks += [place(ahead(o), 1 - core), place(ahead(o), core)]
+        dkeys = pair_dot(jnp.concatenate([ds_ref[b] for b in blocks], axis=0), q_ref[...])
+        dvals = pair_dot(jnp.concatenate([pb_ref[b] for b in blocks], axis=0), diffb[...])
+        for i, o in enumerate(batch):
+            a = 2 * i * per
+            gsib_out[o, :, 0:width] = dkeys[a:a + per]
+            gsib_out[o, :, width:] = dvals[a:a + per]
+            send(gsib_out.at[o], gsib_in.at[o], gs_send.at[o], gs_recv.at[o], sibling)
+            gmine[o, :, 0:width] = dkeys[a + per:a + 2 * per]
+            gmine[o, :, width:] = dvals[a + per:a + 2 * per]
+
+    def finish(batch):
+        for o in batch:
+            arrived(gsib_in.at[o], gs_send.at[o], gs_recv.at[o])
+            if o > 0:
+                gout[o] = (gmine[o] + gsib_in[o]).astype(jnp.bfloat16)
+                send(gout.at[o], gin.at[o], g_send.at[o], g_recv.at[o], peer(ahead(o)))
+
+    for i, batch in enumerate(batches):
+        produce(batch)
+        if i > 0:
+            finish(batches[i - 1])
+        if i == 0:
+            arrived(sq_sib, sq_send.at[0], sq_recv.at[0])
+            sq_chip[...] = sq_own[...] + sq_sib[...]
+            for o in range(1, n_flat):
+                send(sq_chip, sq_in.at[o], sq_send.at[o], sq_recv.at[o], peer(ahead(o)))
+    finish(batches[-1])
+
+    total = gmine[0] + gsib_in[0]
+    squares = sq_chip[...]
+    for o in range(1, n_flat):
+        arrived(sq_in.at[o], sq_send.at[o], sq_recv.at[o])
+        squares = squares + sq_in[o]
+    loss_ref[0] = jnp.sum(squares) * (1.0 / (rows * n_keys * n_qry))
+    for o in range(1, n_flat):
+        arrived(gin.at[o], g_send.at[o], g_recv.at[o])
+        total = total + gin[o].astype(jnp.float32)
+    new_first = 0.9 * first_ref[...] + 0.1 * total
+    new_second = 0.95 * second_ref[...] + 0.05 * total * total
+    grad_ref[...] = total
+    nfirst_ref[...] = new_first
+    nsecond_ref[...] = new_second
+    params_ref[...] = slot_ref[...] - 0.02 * new_first / (jnp.sqrt(new_second) + 1e-08)
+    for copy in pending:
+        copy.wait_send()
+
+
+def fused(
+    queries, cache_keys, cache_values, entry, visits, doc_length, slot_params,
+    first_moment, second_moment,
+):
+    n_keys = lax.axis_size("keys")
+    n_qry = lax.axis_size("qry")
+    n_flat = n_keys // 2 * n_qry
+    n_blocks = n_keys * n_qry
+    tok, heads, width = queries.shape
+    rows = tok * heads
+    per, wide = slot_params.shape
+    shard_len = cache_keys.shape[0]
+    n_slots = per * n_blocks
+    f32, bf16 = jnp.float32, jnp.bfloat16
+    vmem = pl.BlockSpec(memory_space=pltpu.VMEM)
+    smem = pl.BlockSpec(memory_space=pltpu.SMEM)
+    dma = pltpu.SemaphoreType.DMA
+    owned = jax.ShapeDtypeStruct((per, wide), f32)
+    flops = 2 * rows * width * (2 * n_keys * shard_len + 5 * n_slots)
+    out = pl.pallas_call(
+        functools.partial(step_kernel, n_keys, n_qry),
+        out_shape=(
+            jax.ShapeDtypeStruct((rows, width), bf16),
+            owned, owned, owned, owned,
+            jax.ShapeDtypeStruct((1,), f32),
+        ),
+        in_specs=[smem] * 3 + [vmem] * 6,
+        out_specs=(vmem,) * 5 + (smem,),
+        scratch_shapes=[
+            pltpu.VMEM((n_keys - 1, shard_len, width), bf16),
+            pltpu.VMEM((n_keys - 1, shard_len, width), bf16),
+            pltpu.VMEM((n_blocks, per, wide), bf16),
+            pltpu.VMEM((rows, width), f32),
+            pltpu.VMEM((rows, 2 * width), f32),
+            pltpu.VMEM((n_blocks, per, rows), f32),
+            pltpu.VMEM((n_blocks, per, rows), bf16),
+            pltpu.VMEM((n_blocks, per, rows), bf16),
+            pltpu.VMEM((rows, width), f32),
+            pltpu.VMEM((rows, width), bf16),
+            pltpu.VMEM((n_flat, per, wide), f32),
+            pltpu.VMEM((n_flat, per, wide), f32),
+            pltpu.VMEM((n_flat, per, wide), f32),
+            pltpu.VMEM((n_flat, per, wide), bf16),
+            pltpu.VMEM((n_flat, per, wide), bf16),
+            pltpu.VMEM((8, width), f32),
+            pltpu.VMEM((8, width), f32),
+            pltpu.VMEM((8, width), f32),
+            pltpu.VMEM((n_flat, 8, width), f32),
+            dma((2 * (n_keys - 1),)),
+            dma((2 * (n_keys - 1),)),
+            dma((2 * n_flat - 1,)),
+            dma((2 * n_flat - 1,)),
+            dma((n_flat,)),
+            dma((n_flat,)),
+            dma((n_flat,)),
+            dma((n_flat,)),
+            dma((n_flat,)),
+            dma((n_flat,)),
+        ],
+        compiler_params=pltpu.CompilerParams(
+            collective_id=0, has_side_effects=True, vmem_limit_bytes=48 * 2**20
+        ),
+        cost_estimate=pl.CostEstimate(
+            flops=flops, bytes_accessed=4 * rows * width, transcendentals=rows * n_slots
+        ),
+    )(
+        entry, visits, doc_length, queries.reshape(rows, width), cache_keys, cache_values,
+        slot_params, first_moment, second_moment,
+    )
+    return (out[0].reshape(tok, heads, width),) + tuple(out[1:])
+
+
+def body(*args):
+    per = args[6].shape[0]
+    if per % 16 == 0 and lax.axis_size("keys") % 2 == 0:
+        return fused(*args)
+    return ringed(*args)
+
+
 def solution(mesh):
     return jax.shard_map(
         body,

time: 163 us -> 47.8 us (0.29)
  blocking collectives: 69.8 us -> 0 us
  Pallas kernels: 0 us -> 34.6 us
  waiting for transfers between devices: 23.5 us -> 0 us
  matrix products: 23.3 us -> 0 us
  between operations: 17.3 us -> 4.41 us
  other arithmetic: 12.6 us -> 0 us
  loops' own time: 6.18 us -> 0 us
  starting transfers between devices: 3.64 us -> 0 us
  local copies, waits for them, and re-layouts: 6.17 us -> 8.49 us
    all_gather x1 -> x0, blocking collectives: 38.8 us -> none  [body(): complete_sum = lax.all_gather(copies, ('keys', 'qry'), axis=0, tiled=True)]
    pallas_call x0 -> x1, Pallas kernels: none -> 34.6 us  [fused(): pl.pallas_call(functools.partial(step_kernel, n_keys, n_qry), out_shape=(...]
    psum x1 -> x0, blocking collectives: 30.9 us -> none  [body(): squares_all = lax.psum(squared_terms, ('keys', 'qry'))]
    reduce_scatter x1 -> x0, waiting for transfers between devices: 23.4 us -> none  [body(): lax.psum_scatter(grad_terms, ('keys', 'qry'), scatter_dimension=0, tiled=...]
    dot_general x26 -> x0, matrix products: 23.3 us -> none  [the longest x12 10.1 us: row_scores(): lax.dot_general(left, right, (((1,), (1,)), ((), ())), preferred_element_...]
    unnamed x14 -> x17, local copies, waits for them, and re-layouts: 0.04 us -> 8.49 us
    another operation x10 -> x0, loops' own time: 6.18 us -> none  [the longest x1 4.07 us: body(): lax.fori_loop(0, shards - 1, turn, (cache_keys, cache_values) + state)]
    lt x8 -> x0, other arithmetic: 5.37 us -> none  [attend(): live = (place < length)[None, :]]
  transfers between devices with their start and end apart: 7 -> 0, of which waited for: 1 -> 0; matrix products, arithmetic and copies ran while one was open for 15% -> 0% of each run, Pallas kernels for 0% -> 0%
where the time goes in v1:
time: 47.8 us; the launch traced here: 47.5 us
  Pallas kernels  34.6 us (72%)
  local copies, waits for them, and re-layouts  8.49 us (18%)
  between operations  4.41 us (9%)
    pallas_call x1, Pallas kernels, fused(): pl.pallas_call(functools.partial(step_kernel, n_keys, n_qry), out_shape=(...  34.6 us
    unnamed x17, local copies, waits for them, and re-layouts  8.49 us

profile of v1, /device:TPU:0, one launch (start us, length us, event | category | flops | bytes accessed | tf_op | source)
XLA Modules:
  0.0 47.5 jit_solution(10875498057072945020)
XLA Ops:
  2.6 0.0 copy-start
  2.6 0.9 %copy-done = bf16[128,8,128]{2,1,0:T(8,128)(2,1)S(1)} copy-done((bf16[128,8,128]{2,1,0:T(8,128)(2,1)S(1)}, bf16[128,8,128]{2,1,0:T(8,128)(2,1)}, u32[]{:S(2)}) %copy-start) | copy-done | bytes 262168
  3.5 0.0 copy-start.1
  3.5 0.9 %copy-done.1 = bf16[512,128]{1,0:T(8,128)(2,1)S(1)} copy-done((bf16[512,128]{1,0:T(8,128)(2,1)S(1)}, bf16[512,128]{1,0:T(8,128)(2,1)}, u32[]{:S(2)}) %copy-start.1) | copy-done | bytes 131096
  4.4 0.0 copy-start.2
  4.4 0.9 %copy-done.2 = bf16[512,128]{1,0:T(8,128)(2,1)S(1)} copy-done((bf16[512,128]{1,0:T(8,128)(2,1)S(1)}, bf16[512,128]{1,0:T(8,128)(2,1)}, u32[]{:S(2)}) %copy-start.2) | copy-done | bytes 131096
  5.3 0.0 copy-start.3
  5.3 0.8 %copy-done.3 = f32[64,256]{1,0:T(8,128)S(1)} copy-done((f32[64,256]{1,0:T(8,128)S(1)}, f32[64,256]{1,0:T(8,128)}, u32[]{:S(2)}) %copy-start.3) | copy-done | bytes 65560
  6.2 0.0 copy-start.4
  6.2 0.8 %copy-done.4 = f32[64,256]{1,0:T(8,128)S(1)} copy-done((f32[64,256]{1,0:T(8,128)S(1)}, f32[64,256]{1,0:T(8,128)}, u32[]{:S(2)}) %copy-start.4) | copy-done | bytes 65560
  7.0 0.0 copy-start.5
  7.0 0.8 %copy-done.5 = f32[64,256]{1,0:T(8,128)S(1)} copy-done((f32[64,256]{1,0:T(8,128)S(1)}, f32[64,256]{1,0:T(8,128)}, u32[]{:S(2)}) %copy-start.5) | copy-done | bytes 65560
  7.8 34.6 %shard_map.136 = (bf16[1024,128]{1,0:T(8,128)(2,1)S(1)}, f32[64,256]{1,0:T(8,128)S(1)}, f32[64,256]{1,0:T(8,128)S(1)}, f32[64,256]{1,0:T(8,128)S(1)}, f32[64,256]{1,0:T(8,128)S(1)}, /*index=5*/f32[1]{0:T(128)}) custom-call(s32[1,1]{1,0:T(1,128)S(6)} %copy.21.entry_ref, s32[1,1]{1,0:T(1,128)S(6)} %copy.22.visits_ref, s32[1]{0:T(128)S(6)} %copy.23.length_ref, ...), custom_call_target="tpu_custom_call" | custom-call | flops 2415919104 | bytes 524288 | tf_op jit(solution)/shard_map/pallas_call | solution.py:449
  42.4 0.7 %copy.24 = bf16[128,8,128]{2,1,0:T(8,128)(2,1)} copy(bf16[128,8,128]{2,1,0:T(8,128)(2,1)S(1)} %bitcast.2) | data formatting | bytes 524288
  43.1 0.6 %copy.25 = f32[64,256]{1,0:T(8,128)} copy(f32[64,256]{1,0:T(8,128)S(1)} %get-tuple-element.25) | data formatting | bytes 131072
  43.8 0.6 %copy.26 = f32[64,256]{1,0:T(8,128)} copy(f32[64,256]{1,0:T(8,128)S(1)} %get-tuple-element.26) | data formatting | bytes 131072
  44.4 0.6 %copy.27 = f32[64,256]{1,0:T(8,128)} copy(f32[64,256]{1,0:T(8,128)S(1)} %get-tuple-element.27) | data formatting | bytes 131072
  45.0 0.6 %copy.28 = f32[64,256]{1,0:T(8,128)} copy(f32[64,256]{1,0:T(8,128)S(1)} %get-tuple-element.28) | data formatting | bytes 131072
Async XLA Ops:
  2.6 1.0 %copy-start = (bf16[128,8,128]{2,1,0:T(8,128)(2,1)S(1)}, bf16[128,8,128]{2,1,0:T(8,128)(2,1)}, u32[]{:S(2)}) copy-start(bf16[128,8,128]{2,1,0:T(8,128)(2,1)} %param.9) | copy-start | bytes 786436
  3.5 0.9 %copy-start.1 = (bf16[512,128]{1,0:T(8,128)(2,1)S(1)}, bf16[512,128]{1,0:T(8,128)(2,1)}, u32[]{:S(2)}) copy-start(bf16[512,128]{1,0:T(8,128)(2,1)} %k_ref.1) | copy-start | bytes 393220
  4.4 0.9 %copy-start.2 = (bf16[512,128]{1,0:T(8,128)(2,1)S(1)}, bf16[512,128]{1,0:T(8,128)(2,1)}, u32[]{:S(2)}) copy-start(bf16[512,128]{1,0:T(8,128)(2,1)} %v_ref.1) | copy-start | bytes 393220
  5.3 0.8 %copy-start.3 = (f32[64,256]{1,0:T(8,128)S(1)}, f32[64,256]{1,0:T(8,128)}, u32[]{:S(2)}) copy-start(f32[64,256]{1,0:T(8,128)} %slot_ref.1) | copy-start | bytes 196612
  6.2 0.8 %copy-start.4 = (f32[64,256]{1,0:T(8,128)S(1)}, f32[64,256]{1,0:T(8,128)}, u32[]{:S(2)}) copy-start(f32[64,256]{1,0:T(8,128)} %first_ref.1) | copy-start | bytes 196612
  7.0 0.8 %copy-start.5 = (f32[64,256]{1,0:T(8,128)S(1)}, f32[64,256]{1,0:T(8,128)}, u32[]{:S(2)}) copy-start(f32[64,256]{1,0:T(8,128)} %second_ref.1) | copy-start | bytes 196612

commit v2 on v1

--- a/solution.py
+++ b/solution.py
@@ -159,18 +159,23 @@
     entry_ref,
     visits_ref,
     length_ref,
+    q_hbm,
+    k_hbm,
+    v_hbm,
+    slot_hbm,
+    first_hbm,
+    second_hbm,
+    teach_hbm,
+    owned_hbm,
+    loss_ref,
+    teach_ref,
+    owned_ref,
     q_ref,
     k_ref,
     v_ref,
     slot_ref,
     first_ref,
     second_ref,
-    teach_ref,
-    grad_ref,
-    params_ref,
-    nfirst_ref,
-    nsecond_ref,
-    loss_ref,
     kbuf,
     vbuf,
     slots,
@@ -190,6 +195,8 @@
     sq_sib,
     sq_chip,
     sq_in,
+    in_sem,
+    out_sem,
     kv_send,
     kv_recv,
     sl_send,
@@ -247,24 +254,35 @@
             device_id=sibling, device_id_type=MESH,
         ).wait_recv()
 
+    loads = [
+        pltpu.make_async_copy(src, dst, in_sem.at[i])
+        for i, (src, dst) in enumerate((
+            (slot_hbm, slot_ref), (q_hbm, q_ref), (k_hbm, k_ref), (v_hbm, v_ref),
+            (first_hbm, first_ref), (second_hbm, second_ref),
+        ))
+    ]
+    for load in loads:
+        load.start()
+
     barrier = pltpu.get_barrier_semaphore()
     pl.semaphore_signal(barrier, inc=1, device_id=sibling, device_id_type=MESH)
     for o in range(1, n_flat):
         pl.semaphore_signal(barrier, inc=1, device_id=peer(ahead(o)), device_id_type=MESH)
     mine = place(flat, core)
+    loads[0].wait()
     slots[mine] = slot_ref[...].astype(jnp.bfloat16)
     pl.semaphore_wait(barrier, n_flat)
 
     send(slots.at[mine], slots.at[mine], sl_send.at[0], sl_recv.at[0], sibling)
-    send(k_ref, kbuf.at[0], kv_send.at[0], kv_recv.at[0], sibling)
-    send(v_ref, vbuf.at[0], kv_send.at[1], kv_recv.at[1], sibling)
+    send(k_hbm, kbuf.at[0], kv_send.at[0], kv_recv.at[0], sibling)
+    send(v_hbm, vbuf.at[0], kv_send.at[1], kv_recv.at[1], sibling)
     for o in range(1, n_flat):
         send(slots.at[mine], slots.at[mine], sl_send.at[o], sl_recv.at[o], peer(ahead(o)))
     for j in range(1, n_x):
         there = (grp, lax.rem(x + j, n_x) * 2 + core, me_q)
         s = 2 * j - 1
-        send(k_ref, kbuf.at[s], kv_send.at[2 * s], kv_recv.at[2 * s], there)
-        send(v_ref, vbuf.at[s], kv_send.at[2 * s + 1], kv_recv.at[2 * s + 1], there)
+        send(k_hbm, kbuf.at[s], kv_send.at[2 * s], kv_recv.at[2 * s], there)
+        send(v_hbm, vbuf.at[s], kv_send.at[2 * s + 1], kv_recv.at[2 * s + 1], there)
 
     start = entry_ref[0, 0]
     count = visits_ref[0, 0]
@@ -297,6 +315,8 @@
 
         lax.fori_loop(0, tiles, one, 0, unroll=2)
 
+    for load in loads[1:4]:
+        load.wait()
     attend(k_ref, v_ref, me_k, True)
     arrived(kbuf.at[0], kv_send.at[0], kv_recv.at[0])
     arrived(vbuf.at[0], kv_send.at[1], kv_recv.at[1])
@@ -354,77 +374,106 @@
         attend(kbuf.at[g], vbuf.at[g], far + 1 - core, False)
 
     sq_own[...] = jnp.zeros_like(sq_own)
-
-    def differ(t, carry):
-        at = pl.ds(pl.multiple_of(t * tile, tile), tile)
+    for t in range(tiles):
+        at = pl.ds(t * tile, tile)
         teacher = (acc[at, 0:width] / acc[at, width:]).astype(jnp.bfloat16)
         teach_ref[at, :] = teacher
         diff = student[at, :] - teacher.astype(jnp.float32)
         sq_own[...] += jnp.sum((diff * diff).reshape(tile // 8, 8, width), axis=0)
-        diff_b = diff.astype(jnp.bfloat16)
-        diffb[at, :] = diff_b
-        dprob = row_scores(slot_values(), diff_b)
+        diffb[at, :] = diff.astype(jnp.bfloat16)
+    write_teach = pltpu.make_async_copy(teach_ref, teach_hbm, out_sem.at[0])
+    write_teach.start()
+    send(sq_own, sq_sib, sq_send.at[0], sq_recv.at[0], sibling)
+
+    order = list(range(1, n_flat)) + [0]
+    group = 2 if n_flat % 2 == 0 else 1
+    batches = n_flat // group
+    VALUES, KEYS = 0, 1
+
+    def produce(half, i):
+        left, right = ((pb_ref, diffb), (ds_ref, q_ref))[half]
+        first = i * group
+        offsets = order[first:first + group]
+        blocks = [place(ahead(o), 1 - core) for o in offsets]
+        blocks += [place(ahead(o), core) for o in offsets]
+        terms = pair_dot(jnp.concatenate([left[b] for b in blocks], axis=0), right[...])
+        terms = terms.reshape(2, group, per, width)
+        span = pl.ds(first, group)
+        gsib_out[half, span] = terms[0]
+        gmine[half, span] = terms[1]
+        sem = half * batches + i
+        send(gsib_out.at[half, span], gsib_in.at[half, span], gs_send.at[sem], gs_recv.at[sem], sibling)
+
+    def finish(half, i):
+        first = i * group
+        sem = half * batches + i
+        arrived(gsib_in.at[half, pl.ds(first, group)], gs_send.at[sem], gs_recv.at[sem])
+        for p in range(first, first + group):
+            o = order[p]
+            if o > 0:
+                gout[half, p] = (gmine[half, p] + gsib_in[half, p]).astype(jnp.bfloat16)
+                i = half * n_flat + p
+                send(gout.at[half, p], gin.at[half, p], g_send.at[i], g_recv.at[i], peer(ahead(o)))
+
+    for i in range(batches):
+        produce(VALUES, i)
+        if i > 0:
+            finish(VALUES, i - 1)
+    finish(VALUES, batches - 1)
+    arrived(sq_sib, sq_send.at[0], sq_recv.at[0])
+    sq_chip[...] = sq_own[...] + sq_sib[...]
+    for o in range(1, n_flat):
+        send(sq_chip, sq_in.at[o], sq_send.at[o], sq_recv.at[o], peer(ahead(o)))
+
+    for t in range(tiles):
+        at = pl.ds(t * tile, tile)
+        dprob = row_scores(slot_values(), diffb[at, :])
         prob = e_ref[:, :, at].reshape(n_slots, tile)
         inner = jnp.sum(prob * dprob, axis=0, keepdims=True)
         ds_ref[:, :, at] = grouped((prob * (dprob - inner) * scale).astype(jnp.bfloat16))
-        return carry
-
-    lax.fori_loop(0, tiles, differ, 0)
-    send(sq_own, sq_sib, sq_send.at[0], sq_recv.at[0], sibling)
-
-    order = list(range(1, n_flat)) + [0]
-    group = 2 if n_flat % 2 == 0 else 1
-    batches = [order[i:i + group] for i in range(0, n_flat, group)]
-
-    def produce(batch):
-        blocks = []
-        for o in batch:
-            blocks += [place(ahead(o), 1 - core), place(ahead(o), core)]
-        dkeys = pair_dot(jnp.concatenate([ds_ref[b] for b in blocks], axis=0), q_ref[...])
-        dvals = pair_dot(jnp.concatenate([pb_ref[b] for b in blocks], axis=0), diffb[...])
-        for i, o in enumerate(batch):
-            a = 2 * i * per
-            gsib_out[o, :, 0:width] = dkeys[a:a + per]
-            gsib_out[o, :, width:] = dvals[a:a + per]
-            send(gsib_out.at[o], gsib_in.at[o], gs_send.at[o], gs_recv.at[o], sibling)
-            gmine[o, :, 0:width] = dkeys[a + per:a + 2 * per]
-            gmine[o, :, width:] = dvals[a + per:a + 2 * per]
-
-    def finish(batch):
-        for o in batch:
-            arrived(gsib_in.at[o], gs_send.at[o], gs_recv.at[o])
-            if o > 0:
-                gout[o] = (gmine[o] + gsib_in[o]).astype(jnp.bfloat16)
-                send(gout.at[o], gin.at[o], g_send.at[o], g_recv.at[o], peer(ahead(o)))
-
-    for i, batch in enumerate(batches):
-        produce(batch)
+
+    for i in range(batches):
+        produce(KEYS, i)
         if i > 0:
-            finish(batches[i - 1])
-        if i == 0:
-            arrived(sq_sib, sq_send.at[0], sq_recv.at[0])
-            sq_chip[...] = sq_own[...] + sq_sib[...]
-            for o in range(1, n_flat):
-                send(sq_chip, sq_in.at[o], sq_send.at[o], sq_recv.at[o], peer(ahead(o)))
-    finish(batches[-1])
-
-    total = gmine[0] + gsib_in[0]
+            finish(KEYS, i - 1)
+    finish(KEYS, batches - 1)
+
     squares = sq_chip[...]
     for o in range(1, n_flat):
         arrived(sq_in.at[o], sq_send.at[o], sq_recv.at[o])
         squares = squares + sq_in[o]
     loss_ref[0] = jnp.sum(squares) * (1.0 / (rows * n_keys * n_qry))
-    for o in range(1, n_flat):
-        arrived(gin.at[o], g_send.at[o], g_recv.at[o])
-        total = total + gin[o].astype(jnp.float32)
-    new_first = 0.9 * first_ref[...] + 0.1 * total
-    new_second = 0.95 * second_ref[...] + 0.05 * total * total
-    grad_ref[...] = total
-    nfirst_ref[...] = new_first
-    nsecond_ref[...] = new_second
-    params_ref[...] = slot_ref[...] - 0.02 * new_first / (jnp.sqrt(new_second) + 1e-08)
+    for load in loads[4:]:
+        load.wait()
+    for half in (VALUES, KEYS):
+        total = gmine[half, n_flat - 1] + gsib_in[half, n_flat - 1]
+        for p in range(n_flat - 1):
+            i = half * n_flat + p
+            arrived(gin.at[half, p], g_send.at[i], g_recv.at[i])
+            total = total + gin[half, p].astype(jnp.float32)
+        part = pl.ds(width if half == VALUES else 0, width)
+        new_first = 0.9 * first_ref[:, part] + 0.1 * total
+        new_second = 0.95 * second_ref[:, part] + 0.05 * total * total
+        owned_ref[0, :, part] = total
+        owned_ref[1, :, part] = slot_ref[:, part] - 0.02 * new_first / (jnp.sqrt(new_second) + 1e-08)
+        owned_ref[2, :, part] = new_first
+        owned_ref[3, :, part] = new_second
+    write_owned = pltpu.make_async_copy(owned_ref, owned_hbm, out_sem.at[1])
+    write_owned.start()
+    write_teach.wait()
+    write_owned.wait()
     for copy in pending:
         copy.wait_send()
+
+
+def write_kernel(teach_ref, owned_ref, teach_out, grad_out, params_out, first_out, second_out, sems):
+    copies = [pltpu.make_async_copy(teach_ref, teach_out, sems.at[4])]
+    for i, out in enumerate((grad_out, params_out, first_out, second_out)):
+        copies.append(pltpu.make_async_copy(owned_ref.at[i], out, sems.at[i]))
+    for copy in copies:
+        copy.start()
+    for copy in copies:
+        copy.wait()
 
 
 def fused(
@@ -441,21 +490,29 @@
     shard_len = cache_keys.shape[0]
     n_slots = per * n_blocks
     f32, bf16 = jnp.float32, jnp.bfloat16
-    vmem = pl.BlockSpec(memory_space=pltpu.VMEM)
+    hbm = pl.BlockSpec(memory_space=pltpu.HBM)
     smem = pl.BlockSpec(memory_space=pltpu.SMEM)
     dma = pltpu.SemaphoreType.DMA
     owned = jax.ShapeDtypeStruct((per, wide), f32)
     flops = 2 * rows * width * (2 * n_keys * shard_len + 5 * n_slots)
-    out = pl.pallas_call(
+    teach, stacked, loss = pl.pallas_call(
         functools.partial(step_kernel, n_keys, n_qry),
         out_shape=(
             jax.ShapeDtypeStruct((rows, width), bf16),
-            owned, owned, owned, owned,
+            jax.ShapeDtypeStruct((4, per, wide), f32),
             jax.ShapeDtypeStruct((1,), f32),
         ),
-        in_specs=[smem] * 3 + [vmem] * 6,
-        out_specs=(vmem,) * 5 + (smem,),
+        in_specs=[smem] * 3 + [hbm] * 6,
+        out_specs=(hbm, hbm, smem),
         scratch_shapes=[
+            pltpu.VMEM((rows, width), bf16),
+            pltpu.VMEM((4, per, wide), f32),
+            pltpu.VMEM((rows, width), bf16),
+            pltpu.VMEM((shard_len, width), bf16),
+            pltpu.VMEM((shard_len, width), bf16),
+            pltpu.VMEM((per, wide), f32),
+            pltpu.VMEM((per, wide), f32),
+            pltpu.VMEM((per, wide), f32),
             pltpu.VMEM((n_keys - 1, shard_len, width), bf16),
             pltpu.VMEM((n_keys - 1, shard_len, width), bf16),
             pltpu.VMEM((n_blocks, per, wide), bf16),
@@ -466,28 +523,30 @@
             pltpu.VMEM((n_blocks, per, rows), bf16),
             pltpu.VMEM((rows, width), f32),
             pltpu.VMEM((rows, width), bf16),
-            pltpu.VMEM((n_flat, per, wide), f32),
-            pltpu.VMEM((n_flat, per, wide), f32),
-            pltpu.VMEM((n_flat, per, wide), f32),
-            pltpu.VMEM((n_flat, per, wide), bf16),
-            pltpu.VMEM((n_flat, per, wide), bf16),
+            pltpu.VMEM((2, n_flat, per, width), f32),
+            pltpu.VMEM((2, n_flat, per, width), f32),
+            pltpu.VMEM((2, n_flat, per, width), f32),
+            pltpu.VMEM((2, n_flat, per, width), bf16),
+            pltpu.VMEM((2, n_flat, per, width), bf16),
             pltpu.VMEM((8, width), f32),
             pltpu.VMEM((8, width), f32),
             pltpu.VMEM((8, width), f32),
             pltpu.VMEM((n_flat, 8, width), f32),
+            dma((6,)),
+            dma((2,)),
             dma((2 * (n_keys - 1),)),
             dma((2 * (n_keys - 1),)),
             dma((2 * n_flat - 1,)),
             dma((2 * n_flat - 1,)),
-            dma((n_flat,)),
-            dma((n_flat,)),
-            dma((n_flat,)),
-            dma((n_flat,)),
+            dma((2 * n_flat,)),
+            dma((2 * n_flat,)),
+            dma((2 * n_flat,)),
+            dma((2 * n_flat,)),
             dma((n_flat,)),
             dma((n_flat,)),
         ],
         compiler_params=pltpu.CompilerParams(
-            collective_id=0, has_side_effects=True, vmem_limit_bytes=48 * 2**20
+            collective_id=0, has_side_effects=True, vmem_limit_bytes=63 * 2**20
         ),
         cost_estimate=pl.CostEstimate(
             flops=flops, bytes_accessed=4 * rows * width, transcendentals=rows * n_slots
@@ -496,7 +555,15 @@
         entry, visits, doc_length, queries.reshape(rows, width), cache_keys, cache_values,
         slot_params, first_moment, second_moment,
     )
-    return (out[0].reshape(tok, heads, width),) + tuple(out[1:])
+    out = pl.pallas_call(
+        write_kernel,
+        out_shape=(jax.ShapeDtypeStruct((rows, width), bf16), owned, owned, owned, owned),
+        in_specs=[hbm, hbm],
+        out_specs=(hbm,) * 5,
+        scratch_shapes=[dma((5,))],
+        compiler_params=pltpu.CompilerParams(vmem_limit_bytes=63 * 2**20),
+    )(teach, stacked)
+    return (out[0].reshape(tok, heads, width),) + tuple(out[1:]) + (loss,)
 
 
 def body(*args):

time: 47.8 us -> 56.8 us (1.19)
  Pallas kernels: 34.6 us -> 52.3 us
  local copies, waits for them, and re-layouts: 8.49 us -> 0 us
    pallas_call x0 -> x1, Pallas kernels: none -> 17 us  [fused(): pl.pallas_call(write_kernel, out_shape=(jax.ShapeDtypeStruct((rows, width...]
    unnamed x17 -> x0, local copies, waits for them, and re-layouts: 8.49 us -> none
    pallas_call x1, Pallas kernels: 34.6 us -> 35.3 us  [fused(): pl.pallas_call(functools.partial(step_kernel, n_keys, n_qry), out_shape=(...]
where the time goes in v2:
time: 56.8 us; the launch traced here: 56.6 us
  Pallas kernels  52.3 us (92%)
  between operations  4.34 us (8%)
    pallas_call x1, Pallas kernels, fused(): pl.pallas_call(functools.partial(step_kernel, n_keys, n_qry), out_shape=(...  35.3 us
    pallas_call x1, Pallas kernels, fused(): pl.pallas_call(write_kernel, out_shape=(jax.ShapeDtypeStruct((rows, width...  17 us

profile of v2, /device:TPU:0, one launch (start us, length us, event | category | flops | bytes accessed | tf_op | source)
XLA Modules:
  0.0 56.6 jit_solution(2798238198579783418)
XLA Ops:
  2.6 35.3 %shard_map.136 = (bf16[1024,128]{1,0:T(8,128)(2,1)}, f32[4,64,256]{2,1,0:T(8,128)}, f32[1]{0:T(128)}) custom-call(s32[1,1]{1,0:T(1,128)S(6)} %copy.16.entry_ref, s32[1,1]{1,0:T(1,128)S(6)} %copy.17.visits_ref, s32[1]{0:T(128)S(6)} %copy.18.length_ref, bf16[1024,128]{1,0:T(8,128)(2,1)} %bitcast.2, bf16[512,128]{1,0:T(8,128)(2,1)} %k_hbm.1, ...), custom_call_target="tpu_custom_call" | custom-call | flops 2415919104 | bytes 524288 | tf_op jit(solution)/shard_map/pallas_call | solution.py:498
  37.8 17.0 %shard_map.137 = (bf16[1024,128]{1,0:T(8,128)(2,1)}, f32[64,256]{1,0:T(8,128)}, f32[64,256]{1,0:T(8,128)}, f32[64,256]{1,0:T(8,128)}, f32[64,256]{1,0:T(8,128)}) custom-call(bf16[1024,128]{1,0:T(8,128)(2,1)} %get-tuple-element.14.teach_ref, f32[4,64,256]{2,1,0:T(8,128)} %get-tuple-element.15.owned_ref), custom_call_target="tpu_custom_call" | custom-call | tf_op jit(solution)/shard_map/pallas_call | solution.py:558

commit v3 on v2

--- a/solution.py
+++ b/solution.py
@@ -191,9 +191,12 @@
     gsib_in,
     gout,
     gin,
+    zout,
+    zin,
     sq_own,
     sq_sib,
     sq_chip,
+    sq_row,
     sq_in,
     in_sem,
     out_sem,
@@ -205,6 +208,8 @@
     gs_recv,
     g_send,
     g_recv,
+    z_send,
+    z_recv,
     sq_send,
     sq_recv,
 ):
@@ -215,7 +220,6 @@
     me_q = lax.axis_index("qry")
     x = lax.div(me_k, 2)
     core = lax.rem(me_k, 2)
-    flat = x * n_qry + me_q
     sibling = (grp, x * 2 + 1 - core, me_q)
     rows, width = q_ref.shape
     shard_len = k_ref.shape[0]
@@ -226,17 +230,20 @@
     tile = math.gcd(rows, 256)
     tiles = rows // tile
 
-    def place(f, c):
-        return (lax.div(f, n_qry) * 2 + c) * n_qry + lax.rem(f, n_qry)
-
-    def peer(f):
-        return (grp, lax.div(f, n_qry) * 2 + core, lax.rem(f, n_qry))
-
-    def ahead(o):
-        return lax.rem(flat + o, n_flat)
-
-    def behind(o):
-        return lax.rem(flat + n_flat - o, n_flat)
+    def place(at_x, c, at_q):
+        return (at_x * 2 + c) * n_qry + at_q
+
+    def on_x(o):
+        return lax.rem(x + o + n_x, n_x)
+
+    def on_q(o):
+        return lax.rem(me_q + o + n_qry, n_qry)
+
+    def x_peer(o):
+        return (grp, on_x(o) * 2 + core, me_q)
+
+    def q_peer(o):
+        return (grp, me_k, on_q(o))
 
     pending = []
 
@@ -266,18 +273,25 @@
 
     barrier = pltpu.get_barrier_semaphore()
     pl.semaphore_signal(barrier, inc=1, device_id=sibling, device_id_type=MESH)
-    for o in range(1, n_flat):
-        pl.semaphore_signal(barrier, inc=1, device_id=peer(ahead(o)), device_id_type=MESH)
-    mine = place(flat, core)
+    for o in range(1, n_x):
+        pl.semaphore_signal(barrier, inc=1, device_id=x_peer(o), device_id_type=MESH)
+    for o in range(1, n_qry):
+        pl.semaphore_signal(barrier, inc=1, device_id=q_peer(o), device_id_type=MESH)
+    mine = place(x, core, me_q)
     loads[0].wait()
     slots[mine] = slot_ref[...].astype(jnp.bfloat16)
-    pl.semaphore_wait(barrier, n_flat)
-
-    send(slots.at[mine], slots.at[mine], sl_send.at[0], sl_recv.at[0], sibling)
+    pl.semaphore_wait(barrier, n_x + n_qry - 1)
+
+    def pass_on(i, block, dev):
+        send(slots.at[block], slots.at[block], sl_send.at[i], sl_recv.at[i], dev)
+
+    for o in range(1, n_x):
+        pass_on(o * n_qry, mine, x_peer(o))
+    for o in range(1, n_qry):
+        pass_on(o, mine, q_peer(o))
+    pass_on(n_flat, mine, sibling)
     send(k_hbm, kbuf.at[0], kv_send.at[0], kv_recv.at[0], sibling)
     send(v_hbm, vbuf.at[0], kv_send.at[1], kv_recv.at[1], sibling)
-    for o in range(1, n_flat):
-        send(slots.at[mine], slots.at[mine], sl_send.at[o], sl_recv.at[o], peer(ahead(o)))
     for j in range(1, n_x):
         there = (grp, lax.rem(x + j, n_x) * 2 + core, me_q)
         s = 2 * j - 1
@@ -318,19 +332,25 @@
     for load in loads[1:4]:
         load.wait()
     attend(k_ref, v_ref, me_k, True)
+    for o in range(1, n_x):
+        block = place(on_x(-o), core, me_q)
+        arrived(slots.at[block], sl_send.at[o * n_qry], sl_recv.at[o * n_qry])
+        for z in range(1, n_qry):
+            pass_on(o * n_qry + z, block, q_peer(z))
+        pass_on(n_flat + o * n_qry, block, sibling)
     arrived(kbuf.at[0], kv_send.at[0], kv_recv.at[0])
     arrived(vbuf.at[0], kv_send.at[1], kv_recv.at[1])
     attend(kbuf.at[0], vbuf.at[0], x * 2 + 1 - core, False)
-
-    for o in range(1, n_flat):
-        block = place(behind(o), core)
-        arrived(slots.at[block], sl_send.at[o], sl_recv.at[o])
-        i = n_flat - 1 + o
-        send(slots.at[block], slots.at[block], sl_send.at[i], sl_recv.at[i], sibling)
-    arrived(slots.at[place(flat, 1 - core)], sl_send.at[0], sl_recv.at[0])
-    for o in range(1, n_flat):
-        i = n_flat - 1 + o
-        arrived(slots.at[place(behind(o), 1 - core)], sl_send.at[i], sl_recv.at[i])
+    for o in range(n_x):
+        for z in range(1, n_qry):
+            i = o * n_qry + z
+            block = place(on_x(-o), core, on_q(-z))
+            arrived(slots.at[block], sl_send.at[i], sl_recv.at[i])
+            pass_on(n_flat + i, block, sibling)
+    for o in range(n_x):
+        for z in range(n_qry):
+            i = n_flat + o * n_qry + z
+            arrived(slots.at[place(on_x(-o), 1 - core, on_q(-z))], sl_send.at[i], sl_recv.at[i])
 
     def slot_keys():
         return slots[:, :, 0:width].reshape(n_slots, width)
@@ -385,45 +405,44 @@
     write_teach.start()
     send(sq_own, sq_sib, sq_send.at[0], sq_recv.at[0], sibling)
 
-    order = list(range(1, n_flat)) + [0]
-    group = 2 if n_flat % 2 == 0 else 1
-    batches = n_flat // group
     VALUES, KEYS = 0, 1
 
-    def produce(half, i):
+    def produce(half):
         left, right = ((pb_ref, diffb), (ds_ref, q_ref))[half]
-        first = i * group
-        offsets = order[first:first + group]
-        blocks = [place(ahead(o), 1 - core) for o in offsets]
-        blocks += [place(ahead(o), core) for o in offsets]
-        terms = pair_dot(jnp.concatenate([left[b] for b in blocks], axis=0), right[...])
-        terms = terms.reshape(2, group, per, width)
-        span = pl.ds(first, group)
-        gsib_out[half, span] = terms[0]
-        gmine[half, span] = terms[1]
-        sem = half * batches + i
-        send(gsib_out.at[half, span], gsib_in.at[half, span], gs_send.at[sem], gs_recv.at[sem], sibling)
-
-    def finish(half, i):
-        first = i * group
-        sem = half * batches + i
-        arrived(gsib_in.at[half, pl.ds(first, group)], gs_send.at[sem], gs_recv.at[sem])
-        for p in range(first, first + group):
-            o = order[p]
-            if o > 0:
-                gout[half, p] = (gmine[half, p] + gsib_in[half, p]).astype(jnp.bfloat16)
-                i = half * n_flat + p
-                send(gout.at[half, p], gin.at[half, p], g_send.at[i], g_recv.at[i], peer(ahead(o)))
-
-    for i in range(batches):
-        produce(VALUES, i)
-        if i > 0:
-            finish(VALUES, i - 1)
-    finish(VALUES, batches - 1)
+        for o in list(range(1, n_x)) + [0]:
+            for c, to in ((1 - core, gsib_out), (core, gmine)):
+                block = left[pl.ds(place(on_x(o), c, 0), n_qry)].reshape(n_qry * per, rows)
+                to[half, o] = pair_dot(block, right[...]).reshape(n_qry, per, width)
+                if to is gsib_out:
+                    sem = half * n_x + o
+                    send(gsib_out.at[half, o], gsib_in.at[half, o], gs_send.at[sem], gs_recv.at[sem], sibling)
+
+    def to_x(half):
+        for o in range(1, n_x):
+            sem = half * n_x + o
+            arrived(gsib_in.at[half, o], gs_send.at[sem], gs_recv.at[sem])
+            gout[half, o] = (gmine[half, o] + gsib_in[half, o]).astype(jnp.bfloat16)
+            send(gout.at[half, o], gin.at[half, o], g_send.at[sem], g_recv.at[sem], x_peer(o))
+
+    def to_z(half):
+        arrived(gsib_in.at[half, 0], gs_send.at[half * n_x], gs_recv.at[half * n_x])
+        total = gmine[half, 0] + gsib_in[half, 0]
+        for o in range(1, n_x):
+            sem = half * n_x + o
+            arrived(gin.at[half, o], g_send.at[sem], g_recv.at[sem])
+            total = total + gin[half, o].astype(jnp.float32)
+        gmine[half, 0] = total
+        zout[half] = total.astype(jnp.bfloat16)
+        for o in range(1, n_qry):
+            sem = half * n_qry + o
+            send(zout.at[half, on_q(o)], zin.at[half, o], z_send.at[sem], z_recv.at[sem], q_peer(o))
+
+    produce(VALUES)
+    to_x(VALUES)
     arrived(sq_sib, sq_send.at[0], sq_recv.at[0])
     sq_chip[...] = sq_own[...] + sq_sib[...]
-    for o in range(1, n_flat):
-        send(sq_chip, sq_in.at[o], sq_send.at[o], sq_recv.at[o], peer(ahead(o)))
+    for o in range(1, n_x):
+        send(sq_chip, sq_in.at[o], sq_send.at[o], sq_recv.at[o], x_peer(o))
 
     for t in range(tiles):
         at = pl.ds(t * tile, tile)
@@ -431,26 +450,33 @@
         prob = e_ref[:, :, at].reshape(n_slots, tile)
         inner = jnp.sum(prob * dprob, axis=0, keepdims=True)
         ds_ref[:, :, at] = grouped((prob * (dprob - inner) * scale).astype(jnp.bfloat16))
-
-    for i in range(batches):
-        produce(KEYS, i)
-        if i > 0:
-            finish(KEYS, i - 1)
-    finish(KEYS, batches - 1)
-
+        if t == tiles // 2:
+            to_z(VALUES)
+
+    produce(KEYS)
+    to_x(KEYS)
     squares = sq_chip[...]
-    for o in range(1, n_flat):
+    for o in range(1, n_x):
         arrived(sq_in.at[o], sq_send.at[o], sq_recv.at[o])
         squares = squares + sq_in[o]
+    sq_row[...] = squares
+    for o in range(1, n_qry):
+        i = n_x - 1 + o
+        send(sq_row, sq_in.at[i], sq_send.at[i], sq_recv.at[i], q_peer(o))
+    to_z(KEYS)
+    for o in range(1, n_qry):
+        i = n_x - 1 + o
+        arrived(sq_in.at[i], sq_send.at[i], sq_recv.at[i])
+        squares = squares + sq_in[i]
     loss_ref[0] = jnp.sum(squares) * (1.0 / (rows * n_keys * n_qry))
     for load in loads[4:]:
         load.wait()
     for half in (VALUES, KEYS):
-        total = gmine[half, n_flat - 1] + gsib_in[half, n_flat - 1]
-        for p in range(n_flat - 1):
-            i = half * n_flat + p
-            arrived(gin.at[half, p], g_send.at[i], g_recv.at[i])
-            total = total + gin[half, p].astype(jnp.float32)
+        total = gmine[half, 0, me_q]
+        for o in range(1, n_qry):
+            i = half * n_qry + o
+            arrived(zin.at[half, o], z_send.at[i], z_recv.at[i])
+            total = total + zin[half, o].astype(jnp.float32)
         part = pl.ds(width if half == VALUES else 0, width)
         new_first = 0.9 * first_ref[:, part] + 0.1 * total
         new_second = 0.95 * second_ref[:, part] + 0.05 * total * total
@@ -466,12 +492,21 @@
         copy.wait_send()
 
 
-def write_kernel(teach_ref, owned_ref, teach_out, grad_out, params_out, first_out, second_out, sems):
-    copies = [pltpu.make_async_copy(teach_ref, teach_out, sems.at[4])]
-    for i, out in enumerate((grad_out, params_out, first_out, second_out)):
-        copies.append(pltpu.make_async_copy(owned_ref.at[i], out, sems.at[i]))
+def write_kernel(teach_hbm, owned_hbm, teach_out, grad_out, params_out, first_out, second_out, teach, owned, sems):
+    load_owned = pltpu.make_async_copy(owned_hbm, owned, sems.at[5])
+    load_teach = pltpu.make_async_copy(teach_hbm, teach, sems.at[6])
+    load_owned.start()
+    load_teach.start()
+    load_owned.wait()
+    copies = [
+        pltpu.make_async_copy(owned.at[i], out, sems.at[i])
+        for i, out in enumerate((grad_out, params_out, first_out, second_out))
+    ]
     for copy in copies:
         copy.start()
+    load_teach.wait()
+    copies.append(pltpu.make_async_copy(teach, teach_out, sems.at[4]))
+    copies[4].start()
     for copy in copies:
         copy.wait()
 
@@ -482,7 +517,8 @@
 ):
     n_keys = lax.axis_size("keys")
     n_qry = lax.axis_size("qry")
-    n_flat = n_keys // 2 * n_qry
+    n_x = n_keys // 2
+    n_flat = n_x * n_qry
     n_blocks = n_keys * n_qry
     tok, heads, width = queries.shape
     rows = tok * heads
@@ -523,27 +559,32 @@
             pltpu.VMEM((n_blocks, per, rows), bf16),
             pltpu.VMEM((rows, width), f32),
             pltpu.VMEM((rows, width), bf16),
-            pltpu.VMEM((2, n_flat, per, width), f32),
-            pltpu.VMEM((2, n_flat, per, width), f32),
-            pltpu.VMEM((2, n_flat, per, width), f32),
-            pltpu.VMEM((2, n_flat, per, width), bf16),
-            pltpu.VMEM((2, n_flat, per, width), bf16),
+            pltpu.VMEM((2, n_x, n_qry, per, width), f32),
+            pltpu.VMEM((2, n_x, n_qry, per, width), f32),
+            pltpu.VMEM((2, n_x, n_qry, per, width), f32),
+            pltpu.VMEM((2, n_x, n_qry, per, width), bf16),
+            pltpu.VMEM((2, n_x, n_qry, per, width), bf16),
+            pltpu.VMEM((2, n_qry, per, width), bf16),
+            pltpu.VMEM((2, n_qry, per, width), bf16),
             pltpu.VMEM((8, width), f32),
             pltpu.VMEM((8, width), f32),
             pltpu.VMEM((8, width), f32),
-            pltpu.VMEM((n_flat, 8, width), f32),
+            pltpu.VMEM((8, width), f32),
+            pltpu.VMEM((n_x + n_qry, 8, width), f32),
             dma((6,)),
             dma((2,)),
             dma((2 * (n_keys - 1),)),
             dma((2 * (n_keys - 1),)),
-            dma((2 * n_flat - 1,)),
-            dma((2 * n_flat - 1,)),
             dma((2 * n_flat,)),
             dma((2 * n_flat,)),
-            dma((2 * n_flat,)),
-            dma((2 * n_flat,)),
-            dma((n_flat,)),
-            dma((n_flat,)),
+            dma((2 * n_x,)),
+            dma((2 * n_x,)),
+            dma((2 * n_x,)),
+            dma((2 * n_x,)),
+            dma((2 * n_qry,)),
+            dma((2 * n_qry,)),
+            dma((n_x + n_qry,)),
+            dma((n_x + n_qry,)),
         ],
         compiler_params=pltpu.CompilerParams(
             collective_id=0, has_side_effects=True, vmem_limit_bytes=63 * 2**20
@@ -560,7 +601,7 @@
         out_shape=(jax.ShapeDtypeStruct((rows, width), bf16), owned, owned, owned, owned),
         in_specs=[hbm, hbm],
         out_specs=(hbm,) * 5,
-        scratch_shapes=[dma((5,))],
+        scratch_shapes=[pltpu.VMEM((rows, width), bf16), pltpu.VMEM((4, per, wide), f32), dma((7,))],
         compiler_params=pltpu.CompilerParams(vmem_limit_bytes=63 * 2**20),
     )(teach, stacked)
     return (out[0].reshape(tok, heads, width),) + tuple(out[1:]) + (loss,)

time: 56.8 us -> 44.8 us (0.79)
  Pallas kernels: 52.3 us -> 40.2 us
    pallas_call x1, Pallas kernels: 17 us -> 1.8 us  [fused(): pl.pallas_call(write_kernel, out_shape=(jax.ShapeDtypeStruct((rows, width...]
    pallas_call x1, Pallas kernels: 35.3 us -> 38.4 us  [fused(): pl.pallas_call(functools.partial(step_kernel, n_keys, n_qry), out_shape=(...]
where the time goes in v3:
time: 44.8 us; the launch traced here: 44.6 us
  Pallas kernels  40.2 us (90%)
  between operations  4.34 us (10%)
    pallas_call x1, Pallas kernels, fused(): pl.pallas_call(functools.partial(step_kernel, n_keys, n_qry), out_shape=(...  38.4 us
    pallas_call x1, Pallas kernels, fused(): pl.pallas_call(write_kernel, out_shape=(jax.ShapeDtypeStruct((rows, width...  1.8 us

profile of v3, /device:TPU:0, one launch (start us, length us, event | category | flops | bytes accessed | tf_op | source)
XLA Modules:
  0.0 44.6 jit_solution(2742266984969838145)
XLA Ops:
  2.6 38.4 %shard_map.136 = (bf16[1024,128]{1,0:T(8,128)(2,1)}, f32[4,64,256]{2,1,0:T(8,128)}, f32[1]{0:T(128)}) custom-call(s32[1,1]{1,0:T(1,128)S(6)} %copy.16.entry_ref, s32[1,1]{1,0:T(1,128)S(6)} %copy.17.visits_ref, s32[1]{0:T(128)S(6)} %copy.18.length_ref, bf16[1024,128]{1,0:T(8,128)(2,1)} %bitcast.2, bf16[512,128]{1,0:T(8,128)(2,1)} %k_hbm.1, ...), custom_call_target="tpu_custom_call" | custom-call | flops 2415919104 | bytes 524288 | tf_op jit(solution)/shard_map/pallas_call | solution.py:534
  41.0 1.8 %shard_map.137 = (bf16[1024,128]{1,0:T(8,128)(2,1)}, f32[64,256]{1,0:T(8,128)}, f32[64,256]{1,0:T(8,128)}, f32[64,256]{1,0:T(8,128)}, f32[64,256]{1,0:T(8,128)}) custom-call(bf16[1024,128]{1,0:T(8,128)(2,1)} %get-tuple-element.14.teach_hbm, f32[4,64,256]{2,1,0:T(8,128)} %get-tuple-element.15.owned_hbm), custom_call_target="tpu_custom_call" | custom-call | tf_op jit(solution)/shard_map/pallas_call | solution.py:599

commit v4 on v2

--- a/solution.py
+++ b/solution.py
@@ -167,9 +167,10 @@
     second_hbm,
     teach_hbm,
     owned_hbm,
-    loss_ref,
+    loss_hbm,
     teach_ref,
     owned_ref,
+    loss_ref,
     q_ref,
     k_ref,
     v_ref,
@@ -284,6 +285,8 @@
         send(k_hbm, kbuf.at[s], kv_send.at[2 * s], kv_recv.at[2 * s], there)
         send(v_hbm, vbuf.at[s], kv_send.at[2 * s + 1], kv_recv.at[2 * s + 1], there)
 
+    for load in loads[1:4]:
+        load.wait()
     start = entry_ref[0, 0]
     count = visits_ref[0, 0]
     length = length_ref[0]
@@ -295,8 +298,8 @@
         limit = jnp.where(turn < count, length, 0)
         bias = jnp.where(col < limit, 0.0, NEG)
 
-        def one(t, carry):
-            at = pl.ds(pl.multiple_of(t * tile, tile), tile)
+        for t in range(tiles):
+            at = pl.ds(t * tile, tile)
             score = row_scores(q_ref[at, :], keys_ref[...]) + bias
             peak = jnp.max(score, axis=1, keepdims=True)
             values = jnp.concatenate([values_ref[...], ones], axis=1)
@@ -311,12 +314,7 @@
                 fade = jnp.exp2((old - new) * rate)
                 acc[at, :] = acc[at, :] * fade + pair_dot(weight.astype(jnp.bfloat16), values)
             top[at, :] = jnp.broadcast_to(new, (tile, width))
-            return carry
-
-        lax.fori_loop(0, tiles, one, 0, unroll=2)
-
-    for load in loads[1:4]:
-        load.wait()
+
     attend(k_ref, v_ref, me_k, True)
     arrived(kbuf.at[0], kv_send.at[0], kv_recv.at[0])
     arrived(vbuf.at[0], kv_send.at[1], kv_recv.at[1])
@@ -343,8 +341,8 @@
 
     values_t = slot_values().astype(jnp.float32).T.astype(jnp.bfloat16)
 
-    def softmax(t, carry):
-        at = pl.ds(pl.multiple_of(t * tile, tile), tile)
+    for t in range(tiles):
+        at = pl.ds(t * tile, tile)
         score = row_scores(slot_keys(), q_ref[at, :])
         peak = jnp.max(score, axis=0, keepdims=True)
         weight = jnp.exp2((score - peak) * rate)
@@ -353,9 +351,6 @@
         prob_b = prob.astype(jnp.bfloat16)
         pb_ref[:, :, at] = grouped(prob_b)
         student[at, :] = pair_dot(values_t, prob_b).T
-        return carry
-
-    lax.fori_loop(0, tiles, softmax, 0)
 
     for j in range(1, n_x):
         s = 2 * j - 1
@@ -442,7 +437,10 @@
     for o in range(1, n_flat):
         arrived(sq_in.at[o], sq_send.at[o], sq_recv.at[o])
         squares = squares + sq_in[o]
-    loss_ref[0] = jnp.sum(squares) * (1.0 / (rows * n_keys * n_qry))
+    loss = jnp.sum(squares, keepdims=True) * (1.0 / (rows * n_keys * n_qry))
+    loss_ref[...] = jnp.broadcast_to(loss, loss_ref.shape)
+    write_loss = pltpu.make_async_copy(loss_ref, loss_hbm, out_sem.at[2])
+    write_loss.start()
     for load in loads[4:]:
         load.wait()
     for half in (VALUES, KEYS):
@@ -462,16 +460,33 @@
     write_owned.start()
     write_teach.wait()
     write_owned.wait()
+    write_loss.wait()
     for copy in pending:
         copy.wait_send()
 
 
-def write_kernel(teach_ref, owned_ref, teach_out, grad_out, params_out, first_out, second_out, sems):
-    copies = [pltpu.make_async_copy(teach_ref, teach_out, sems.at[4])]
-    for i, out in enumerate((grad_out, params_out, first_out, second_out)):
-        copies.append(pltpu.make_async_copy(owned_ref.at[i], out, sems.at[i]))
+def write_kernel(
+    teach_hbm, owned_hbm, loss_hbm, teach_out, grad_out, params_out, first_out, second_out, loss_out,
+    teach, owned, loss, sems,
+):
+    loads = [
+        pltpu.make_async_copy(src, dst, sems.at[i])
+        for i, (src, dst) in enumerate(((owned_hbm, owned), (teach_hbm, teach), (loss_hbm, loss)))
+    ]
+    for load in loads:
+        load.start()
+    loads[0].wait()
+    copies = [
+        pltpu.make_async_copy(owned.at[i], out, sems.at[3 + i])
+        for i, out in enumerate((grad_out, params_out, first_out, second_out))
+    ]
     for copy in copies:
         copy.start()
+    loads[1].wait()
+    copies.append(pltpu.make_async_copy(teach, teach_out, sems.at[7]))
+    copies[4].start()
+    loads[2].wait()
+    loss_out[0] = jnp.max(loss[...])
     for copy in copies:
         copy.wait()
 
@@ -500,13 +515,14 @@
         out_shape=(
             jax.ShapeDtypeStruct((rows, width), bf16),
             jax.ShapeDtypeStruct((4, per, wide), f32),
-            jax.ShapeDtypeStruct((1,), f32),
+            jax.ShapeDtypeStruct((8, width), f32),
         ),
         in_specs=[smem] * 3 + [hbm] * 6,
-        out_specs=(hbm, hbm, smem),
+        out_specs=(hbm,) * 3,
         scratch_shapes=[
             pltpu.VMEM((rows, width), bf16),
             pltpu.VMEM((4, per, wide), f32),
+            pltpu.VMEM((8, width), f32),
             pltpu.VMEM((rows, width), bf16),
             pltpu.VMEM((shard_len, width), bf16),
             pltpu.VMEM((shard_len, width), bf16),
@@ -533,7 +549,7 @@
             pltpu.VMEM((8, width), f32),
             pltpu.VMEM((n_flat, 8, width), f32),
             dma((6,)),
-            dma((2,)),
+            dma((3,)),
             dma((2 * (n_keys - 1),)),
             dma((2 * (n_keys - 1),)),
             dma((2 * n_flat - 1,)),
@@ -557,13 +573,21 @@
     )
     out = pl.pallas_call(
         write_kernel,
-        out_shape=(jax.ShapeDtypeStruct((rows, width), bf16), owned, owned, owned, owned),
-        in_specs=[hbm, hbm],
-        out_specs=(hbm,) * 5,
-        scratch_shapes=[dma((5,))],
+        out_shape=(
+            jax.ShapeDtypeStruct((rows, width), bf16), owned, owned, owned, owned,
+            jax.ShapeDtypeStruct((1,), f32),
+        ),
+        in_specs=[hbm] * 3,
+        out_specs=(hbm,) * 5 + (smem,),
+        scratch_shapes=[
+            pltpu.VMEM((rows, width), bf16),
+            pltpu.VMEM((4, per, wide), f32),
+            pltpu.VMEM((8, width), f32),
+            dma((8,)),
+        ],
         compiler_params=pltpu.CompilerParams(vmem_limit_bytes=63 * 2**20),
-    )(teach, stacked)
-    return (out[0].reshape(tok, heads, width),) + tuple(out[1:]) + (loss,)
+    )(teach, stacked, loss)
+    return (out[0].reshape(tok, heads, width),) + tuple(out[1:])
 
 
 def body(*args):

time: 56.8 us -> 38 us (0.67)
  Pallas kernels: 52.3 us -> 35.3 us
  between operations: 4.34 us -> 2.58 us
    pallas_call x1, Pallas kernels: 17 us -> 2.32 us  [fused(): pl.pallas_call(write_kernel, out_shape=(jax.ShapeDtypeStruct((rows, width...]
    pallas_call x1, Pallas kernels: 35.3 us -> 33 us  [fused(): pl.pallas_call(functools.partial(step_kernel, n_keys, n_qry), out_shape=(...]
where the time goes in v4:
time: 38 us; the launch traced here: 37.9 us
  Pallas kernels  35.3 us (93%)
  between operations  2.58 us (7%)
    pallas_call x1, Pallas kernels, fused(): pl.pallas_call(functools.partial(step_kernel, n_keys, n_qry), out_shape=(...  33 us
    pallas_call x1, Pallas kernels, fused(): pl.pallas_call(write_kernel, out_shape=(jax.ShapeDtypeStruct((rows, width...  2.32 us

profile of v4, /device:TPU:0, one launch (start us, length us, event | category | flops | bytes accessed | tf_op | source)
XLA Modules:
  0.0 37.9 jit_solution(1041896611939148776)
XLA Ops:
  2.6 33.0 %shard_map.136 = (bf16[1024,128]{1,0:T(8,128)(2,1)}, f32[4,64,256]{2,1,0:T(8,128)}, f32[8,128]{1,0:T(8,128)}) custom-call(s32[1,1]{1,0:T(1,128)S(6)} %copy.15.entry_ref, s32[1,1]{1,0:T(1,128)S(6)} %copy.16.visits_ref, s32[1]{0:T(128)S(6)} %copy.17.length_ref, bf16[1024,128]{1,0:T(8,128)(2,1)} %bitcast.2, bf16[512,128]{1,0:T(8,128)(2,1)} %k_hbm.1, ...), custom_call_target="tpu_custom_call" | custom-call | flops 2415919104 | bytes 524288 | tf_op jit(solution)/shard_map/pallas_call | solution.py:513
  35.5 2.3 %shard_map.137 = (bf16[1024,128]{1,0:T(8,128)(2,1)}, f32[64,256]{1,0:T(8,128)}, f32[64,256]{1,0:T(8,128)}, f32[64,256]{1,0:T(8,128)}, f32[64,256]{1,0:T(8,128)}, /*index=5*/f32[1]{0:T(128)}) custom-call(bf16[1024,128]{1,0:T(8,128)(2,1)} %get-tuple-element.15.teach_hbm, f32[4,64,256]{2,1,0:T(8,128)} %get-tuple-element.16.owned_hbm, ...), custom_call_target="tpu_custom_call" | custom-call | tf_op jit(solution)/shard_map/pallas_call | solution.py:574

commit v5 on v4

--- a/solution.py
+++ b/solution.py
@@ -412,13 +412,6 @@
 
     for i in range(batches):
         produce(VALUES, i)
-        if i > 0:
-            finish(VALUES, i - 1)
-    finish(VALUES, batches - 1)
-    arrived(sq_sib, sq_send.at[0], sq_recv.at[0])
-    sq_chip[...] = sq_own[...] + sq_sib[...]
-    for o in range(1, n_flat):
-        send(sq_chip, sq_in.at[o], sq_send.at[o], sq_recv.at[o], peer(ahead(o)))
 
     for t in range(tiles):
         at = pl.ds(t * tile, tile)
@@ -426,12 +419,20 @@
         prob = e_ref[:, :, at].reshape(n_slots, tile)
         inner = jnp.sum(prob * dprob, axis=0, keepdims=True)
         ds_ref[:, :, at] = grouped((prob * (dprob - inner) * scale).astype(jnp.bfloat16))
+        if t == 0:
+            for i in range(batches):
+                finish(VALUES, i)
+            arrived(sq_sib, sq_send.at[0], sq_recv.at[0])
+            sq_chip[...] = sq_own[...] + sq_sib[...]
+            for o in range(1, n_flat):
+                send(sq_chip, sq_in.at[o], sq_send.at[o], sq_recv.at[o], peer(ahead(o)))
 
     for i in range(batches):
         produce(KEYS, i)
-        if i > 0:
-            finish(KEYS, i - 1)
-    finish(KEYS, batches - 1)
+        if i > 1:
+            finish(KEYS, i - 2)
+    for i in range(max(batches - 2, 0), batches):
+        finish(KEYS, i)
 
     squares = sq_chip[...]
     for o in range(1, n_flat):

time: 38 us -> 36.8 us (0.968)
  Pallas kernels: 35.3 us -> 34 us
    pallas_call x1, Pallas kernels: 33 us -> 31.7 us  [fused(): pl.pallas_call(functools.partial(step_kernel, n_keys, n_qry), out_shape=(...]
where the time goes in v5:
time: 36.8 us; the launch traced here: 36.6 us
  Pallas kernels  34 us (92%)
  between operations  2.58 us (7%)
    pallas_call x1, Pallas kernels, fused(): pl.pallas_call(functools.partial(step_kernel, n_keys, n_qry), out_shape=(...  31.7 us
    pallas_call x1, Pallas kernels, fused(): pl.pallas_call(write_kernel, out_shape=(jax.ShapeDtypeStruct((rows, width...  2.32 us

profile of v5, /device:TPU:0, one launch (start us, length us, event | category | flops | bytes accessed | tf_op | source)
XLA Modules:
  0.0 36.6 jit_solution(15736448101659462117)
XLA Ops:
  2.6 31.7 %shard_map.136 = (bf16[1024,128]{1,0:T(8,128)(2,1)}, f32[4,64,256]{2,1,0:T(8,128)}, f32[8,128]{1,0:T(8,128)}) custom-call(s32[1,1]{1,0:T(1,128)S(6)} %copy.15.entry_ref, s32[1,1]{1,0:T(1,128)S(6)} %copy.16.visits_ref, s32[1]{0:T(128)S(6)} %copy.17.length_ref, bf16[1024,128]{1,0:T(8,128)(2,1)} %bitcast.2, bf16[512,128]{1,0:T(8,128)(2,1)} %k_hbm.1, ...), custom_call_target="tpu_custom_call" | custom-call | flops 2415919104 | bytes 524288 | tf_op jit(solution)/shard_map/pallas_call | solution.py:514
  34.3 2.3 %shard_map.137 = (bf16[1024,128]{1,0:T(8,128)(2,1)}, f32[64,256]{1,0:T(8,128)}, f32[64,256]{1,0:T(8,128)}, f32[64,256]{1,0:T(8,128)}, f32[64,256]{1,0:T(8,128)}, /*index=5*/f32[1]{0:T(128)}) custom-call(bf16[1024,128]{1,0:T(8,128)(2,1)} %get-tuple-element.15.teach_hbm, f32[4,64,256]{2,1,0:T(8,128)} %get-tuple-element.16.owned_hbm, ...), custom_call_target="tpu_custom_call" | custom-call | tf_op jit(solution)/shard_map/pallas_call | solution.py:575
